TPU v7x, 256 devices: a whole 4x4x8 slice. The times are simulated.
256 devices in a mesh: grp: 4 (over x), sub: 64 (over z, y, core).
Axes of the slice: x: 4, y: 4, z: 8, core: 2. Of those that a mesh axis runs over, the one named last changes fastest.
Arguments:
- spectra: float32 [256, 6, 512, 512], P(('grp', 'sub')), may hold values from -0.046875 to 0.046875
- legendre: bfloat16 [512, 128, 512], P('sub'), may hold values from -6 to 6
- degree_counts: int32 [4, 512], replicated, may hold values from 1 to 512, as said below
Outputs:
- forcing: bfloat16 [256, 3, 128, 3072], P(('grp', 'sub'))
Inputs may be any that keep to these rules, and one draw needn't show every extreme that they name: degree_counts[g, i] never exceeds 512 - i; within a group it falls by one from one order to the next until it reaches 1.
All inputs are finite; a program needn't handle non-finite values.
Results may differ from a plain program's by a relative error of at most 0.0064.
Values may be sent and summed in bfloat16 or wider, within the bound.
A program may use at most 128 MiB of HBM per device.

v0:
```python
import math

import jax
import jax.numpy as jnp
from jax import lax
from jax.sharding import PartitionSpec as P

LOWEST_ORDER = 512
NLAT = 1536
LONGITUDE_COUNT = 3072


RADIUS_IN = 0.35 / 0.65
ELSASSER = 0.5


def with_halo(cells, sides, width):
    for axis, dim in sides:
        count = lax.axis_size(axis)
        ends = count - 1
        head = lax.slice_in_dim(cells, 0, width, axis=dim)
        tail = lax.slice_in_dim(cells, cells.shape[dim] - width, cells.shape[dim], axis=dim)
        cells = jnp.concatenate(
            [
                lax.ppermute(tail, axis, [(i, (i + 1) % count) for i in range(ends)]),
                cells,
                lax.ppermute(head, axis, [((i + 1) % count, i) for i in range(ends)]),
            ],
            axis=dim,
        )
    return cells


def forcing_terms(velocity, differ, radius, cos_theta, sin_theta):
    flow_radial = velocity[..., 0, :, :]
    flow_polar = velocity[..., 1, :, :]
    flow_azimuth = velocity[..., 2, :, :]
    cross_radial = -sin_theta * flow_azimuth
    cross_polar = -cos_theta * flow_azimuth
    cross_azimuth = cos_theta * flow_polar + sin_theta * flow_radial
    strength = (RADIUS_IN / radius) ** 3
    field_radial = 2.0 * strength * cos_theta
    field_polar = strength * sin_theta
    aligned = flow_radial * field_radial + flow_polar * field_polar
    squared = field_radial * field_radial + field_polar * field_polar
    force_radial = (
        -cross_radial
        + ELSASSER * (aligned * field_radial - squared * flow_radial)
        - flow_radial * differ[..., 0, :, :]
    )
    force_polar = (
        -cross_polar
        + ELSASSER * (aligned * field_polar - squared * flow_polar)
        - flow_radial * differ[..., 1, :, :]
    )
    force_azimuth = (
        -cross_azimuth - ELSASSER * squared * flow_azimuth - flow_radial * differ[..., 2, :, :]
    )
    return jnp.stack([force_radial, force_polar, force_azimuth], axis=-3).astype(jnp.bfloat16)


def shards(spectra, legendre, degree_counts):
    radial_rows = spectra.shape[0]
    order_total = spectra.shape[2]
    latitudes = legendre.shape[1]
    group_index = lax.axis_index("grp")
    counts = lax.dynamic_index_in_dim(degree_counts, group_index, 0, keepdims=False)
    degree_pos = lax.broadcasted_iota(jnp.int32, (order_total, order_total), 1)
    kept_mask = degree_pos < counts[:, None]
    masked = jnp.where(kept_mask[None, None], spectra, 0.0).astype(jnp.bfloat16)
    result = lax.dot_general(
        lax.all_to_all(masked, "sub", split_axis=2, concat_axis=0, tiled=True),
        legendre,
        (((3,), (2,)), ((2,), (0,))),
        preferred_element_type=jnp.float32,
    )
    fourier = result.astype(jnp.bfloat16)
    returned = lax.all_to_all(fourier, "sub", split_axis=1, concat_axis=0, tiled=True)
    order_values = lax.broadcasted_iota(jnp.int32, (order_total, LONGITUDE_COUNT), 0) + LOWEST_ORDER
    points = lax.broadcasted_iota(jnp.int32, (order_total, LONGITUDE_COUNT), 1)
    phase_int = order_values * points % LONGITUDE_COUNT
    angles = phase_int.astype(jnp.float32) * (2.0 * math.pi / LONGITUDE_COUNT)
    synth_table = jnp.stack([jnp.cos(angles), -jnp.sin(angles)])
    grouped = returned.astype(jnp.float32).reshape(
        order_total, returned.shape[1], 3, 2, returned.shape[3]
    )
    velocity = jnp.einsum("mrcql,qmp->rclp", grouped, synth_table, precision=lax.Precision.HIGH)
    extended = with_halo(velocity, ((("grp", "sub"), 0),), 1)
    shells_total = lax.axis_size(("grp", "sub")) * radial_rows
    first_shell = lax.axis_index(("grp", "sub")) * radial_rows
    shell_ids = first_shell + jnp.arange(radial_rows, dtype=jnp.int32)
    outer_shell = extended[2:]
    inner_shell = extended[:-2]
    at_bottom = (shell_ids == 0)[:, None, None, None]
    at_top = (shell_ids == shells_total - 1)[:, None, None, None]
    differ = jnp.where(
        at_bottom,
        outer_shell - velocity,
        jnp.where(at_top, velocity - inner_shell, 0.5 * (outer_shell - inner_shell)),
    )
    radius = (RADIUS_IN + (shell_ids.astype(jnp.float32) + 0.5) / shells_total)[:, None, None]
    colatitude = (
        math.pi * (jnp.arange(latitudes, dtype=jnp.float32) + (NLAT - latitudes) // 2 + 0.5) / NLAT
    )
    cos_theta = jnp.cos(colatitude)[:, None]
    sin_theta = jnp.sin(colatitude)[:, None]
    return forcing_terms(velocity, differ, radius, cos_theta, sin_theta)


def solution(mesh):
    in_specs = (P(("grp", "sub"), None, None, None), P("sub", None, None), P())
    out_specs = P(("grp", "sub"), None, None, None)
    return jax.shard_map(shards, mesh=mesh, in_specs=in_specs, out_specs=out_specs, check_vma=False)
```

profile of v0, /device:TPU:6, one launch (start us, length us, event | category | flops | bytes accessed | tf_op | source)
XLA Modules:
  0.0 248.7 jit_solution(10813396941199173314)
XLA Ops:
  0.0 0.0 copy-start
  0.0 0.8 constant_dynamic-slice_fusion
  0.8 0.2 iota_compare_fusion
  1.0 7.7 %fusion.3 = bf16[1,6,512,512]{3,1,0,2:T(8,128)(2,1)S(1)} fusion(f32[1,6,512,512]{3,2,1,0:T(8,128)} %param.3, pred[512,512]{1,0:T(8,128)(4,1)S(1)} %iota_compare_fusion), kind=kLoop, calls=%fused_computation.6 | loop fusion | flops 1572864 | bytes 9699328 | tf_op jit(solution)/shard_map/convert_element_type | solution.py:70
  8.7 108.2 %all_to_all.33 = bf16[1,6,512,512]{3,1,0,2:T(8,128)(2,1)S(1)} all-to-all(bf16[1,6,512,512]{3,1,0,2:T(8,128)(2,1)S(1)} %fusion.3), channel_id=1, replica_groups=mesh['grp'=4,'sub'=64] {'sub'}, dimensions={2} | all-to-all | bytes 6291456 | tf_op jit(solution)/shard_map/all_to_all | solution.py:72
  116.9 0.0 copy-done
  116.9 3.6 %fusion.20 = bf16[8,64,6,128]{3,1,2,0:T(8,128)(2,1)S(1)} fusion(bf16[1,6,64,8,512]{4,1,3,2,0:T(8,128)(2,1)S(1)} %bitcast.32, bf16[8,128,512]{2,1,0:T(8,128)(2,1)S(1)} %copy-done), kind=kOutput, calls=%fused_computation.31 | convolution fusion | flops 403046400 | bytes 4980736 | tf_op jit(solution)/shard_map/dot_general | solution.py:71
  120.5 1.4 copy.16
  121.9 5.5 %all-to-all-start.1 = ((bf16[8,64,6,128]{3,0,2,1:T(8,128)(2,1)}), bf16[8,64,6,128]{3,0,2,1:T(8,128)(2,1)S(1)}, u32[]{:S(2)}, u32[]{:S(2)}) async-start(bf16[8,64,6,128]{3,0,2,1:T(8,128)(2,1)} %copy.16), calls=%async_computation.1 | async-start | bytes 1572864 | tf_op jit(solution)/shard_map/all_to_all | solution.py:78
  127.4 28.0 %fusion.8 = (f32[1,512,3072]{2,1,0:T(8,128)}, f32[1,512,3072]{2,1,0:T(8,128)}) fusion(s32[512]{0:T(512)S(1)} %iota_add_fusion), kind=kLoop, calls=%fused_computation.13 | loop fusion | flops 15728640 | bytes 12584960 | tf_op jit(solution)/shard_map/cos | solution.py:83
  155.4 0.0 all-to-all-done.1
  155.4 0.1 copy.17
  155.6 10.8 %fusion.10 = f32[1,3,128,3072]{3,2,1,0:T(8,128)} fusion(bf16[512,3,2,128]{3,0,2,1:T(8,128)(2,1)S(1)} %bitcast.33, f32[1,512,3072]{2,1,0:T(8,128)} %get-tuple-element.10, f32[1,512,3072]{2,1,0:T(8,128)} %get-tuple-element.9), kind=kOutput, calls=%fused_computation.16 | convolution fusion | flops 7250903040 | bytes 18087936 | tf_op jit(solution)/shard_map/mrcql,qmp->rclp/dot_general | solution.py:87
  166.3 6.9 %collective-permute-start = (f32[1,3,128,3072]{3,2,1,0:T(8,128)}, f32[1,3,128,3072]{3,2,1,0:T(8,128)}, u32[]{:S(2)}, u32[]{:S(2)}) collective-permute-start(f32[1,3,128,3072]{3,2,1,0:T(8,128)} %fusion.10), channel_id=1, source_target_pairs={{1,0},{2,1},{3,2},{4,3},{5,4},{6,5},{7,6},{8,7},{9,8},{10,9},{11,1... | collective-permute-start | bytes 14155784 | tf_op jit(solution)/shard_map/ppermute | solution.py:27
  173.3 1.9 collective-permute-start.1
  175.3 0.1 broadcast_multiply_fusion
  175.5 49.7 %collective-permute-done = f32[1,3,128,3072]{3,2,1,0:T(8,128)} collective-permute-done((f32[1,3,128,3072]{3,2,1,0:T(8,128)}, f32[1,3,128,3072]{3,2,1,0:T(8,128)}, u32[]{:S(2)}, u32[]{:S(2)}) %collective-permute-start) | collective-permute-done | bytes 4718624 | tf_op jit(solution)/shard_map/ppermute | solution.py:27
  225.2 8.0 %collective-permute-done.1 = f32[1,3,128,3072]{3,2,1,0:T(8,128)} collective-permute-done((f32[1,3,128,3072]{3,2,1,0:T(8,128)}, f32[1,3,128,3072]{3,2,1,0:T(8,128)}, u32[]{:S(2)}, u32[]{:S(2)}) %collective-permute-start.1) | collective-permute-done | bytes 4718624 | tf_op jit(solution)/shard_map/ppermute | solution.py:25
  233.3 6.7 %select_select_fusion = f32[1,3,128,3072]{3,2,1,0:T(8,128)S(1)} fusion(f32[1,3,128,3072]{3,2,1,0:T(8,128)} %collective-permute-done, f32[1,3,128,3072]{3,2,1,0:T(8,128)} %collective-permute-done.1, f32[1,3,128,3072]{3,2,1,0:T(8,128)} %fusion.10, pred[]{:T(512)S(6)} %eq.11, pred[]{:T(512)S(6)} %eq.10), kind=kLoop, calls=%fused_computation.15 | loop fusion | flops 7077888 | bytes 18874370 | tf_op jit(solution)/shard_map/jit(_where)/select_n | solution.py:96
  240.0 3.2 %fusion.15 = bf16[1,1,128,3072]{3,2,1,0:T(8,128)(2,1)S(1)} fusion(f32[1,3,128,3072]{3,2,1,0:T(8,128)S(1)} %select_select_fusion, f32[1,3,128,3072]{3,2,1,0:T(8,128)} %fusion.10, f32[128]{0:T(128)S(1)} %get-tuple-element.5, f32[128]{0:T(128)S(1)} %get-tuple-element.12, f32[128]{0:T(128)S(1)} %get-tuple-element.11), kind=kLoop, calls=%fused_computation.23 | loop fusion | flops 3538944 | bytes 7079424 | tf_op jit(solution)/shard_map/convert.2
  243.1 3.9 %fusion.19 = (bf16[1,1,128,3072]{3,2,1,0:T(8,128)(2,1)S(1)}, bf16[1,1,128,3072]{3,2,1,0:T(8,128)(2,1)S(1)}) fusion(f32[1,3,128,3072]{3,2,1,0:T(8,128)S(1)} %select_select_fusion, f32[1,3,128,3072]{3,2,1,0:T(8,128)} %fusion.10, f32[128]{0:T(128)S(1)} %get-tuple-element.6, f32[128]{0:T(128)S(1)} %get-tuple-element.13, f32[128]{0:T(128)S(1)} %get-tuple-element.14, ...), kind=kLoop, calls=%fused_computation.29 | loop fusion | flops 9043968 | bytes 9439744 | tf_op jit(solution)/shard_map/convert
  247.0 1.7 pad_maximum_fusion
  (4 shorter events, 0.1 us)
Async XLA Ops:
  0.0 116.9 %copy-start = (bf16[8,128,512]{2,1,0:T(8,128)(2,1)S(1)}, bf16[8,128,512]{2,1,0:T(8,128)(2,1)}, u32[]{:S(2)}) copy-start(bf16[8,128,512]{2,1,0:T(8,128)(2,1)} %param.4) | copy-start | bytes 3145732
  121.9 33.5 %all-to-all-start.1 = ((bf16[8,64,6,128]{3,0,2,1:T(8,128)(2,1)}), bf16[8,64,6,128]{3,0,2,1:T(8,128)(2,1)S(1)}, u32[]{:S(2)}, u32[]{:S(2)}) async-start(bf16[8,64,6,128]{3,0,2,1:T(8,128)(2,1)} %copy.16), calls=%async_computation.1 | async-start | bytes 1572864 | tf_op jit(solution)/shard_map/all_to_all | solution.py:78
  166.3 58.9 %collective-permute-start = (f32[1,3,128,3072]{3,2,1,0:T(8,128)}, f32[1,3,128,3072]{3,2,1,0:T(8,128)}, u32[]{:S(2)}, u32[]{:S(2)}) collective-permute-start(f32[1,3,128,3072]{3,2,1,0:T(8,128)} %fusion.10), channel_id=1, source_target_pairs={{1,0},{2,1},{3,2},{4,3},{5,4},{6,5},{7,6},{8,7},{9,8},{10,9},{11,1... | collective-permute-start | bytes 14155784 | tf_op jit(solution)/shard_map/ppermute | solution.py:27
  173.3 60.0 %collective-permute-start.1 = (f32[1,3,128,3072]{3,2,1,0:T(8,128)}, f32[1,3,128,3072]{3,2,1,0:T(8,128)}, u32[]{:S(2)}, u32[]{:S(2)}) collective-permute-start(f32[1,3,128,3072]{3,2,1,0:T(8,128)} %fusion.10), channel_id=1, source_target_pairs={{0,1},{1,2},{2,3},{3,4},{4,5},{5,6},{6,7},{7,8},{8,9},{9,10},{10,1... | collective-permute-start | bytes 14155784 | tf_op jit(solution)/shard_map/ppermute | solution.py:25
where the time goes:
time: 249 us
  blocking collectives  108 us (43%)
  waiting for transfers between devices  57.8 us (23%)
  other arithmetic  51.5 us (21%)
  matrix products  14.4 us (6%)
  starting transfers between devices  14.4 us (6%)
    all_to_all x1, blocking collectives, shards(): lax.all_to_all(masked, 'sub', split_axis=2, concat_axis=0, tiled=True)  108 us
    ppermute x1, waiting for transfers between devices, with_halo(): lax.ppermute(head, axis, [((i + 1) % count, i) for i in range(ends)])  49.7 us
    cos x1, other arithmetic, shards(): synth_table = jnp.stack([jnp.cos(angles), -jnp.sin(angles)])  28 us
    dot_general x1, matrix products, shards(): jnp.einsum('mrcql,qmp->rclp', grouped, synth_table, precision=lax.Precisi...  10.8 us
    ppermute x1, waiting for transfers between devices, with_halo(): lax.ppermute(tail, axis, [(i, (i + 1) % count) for i in range(ends)])  8.04 us
    convert_element_type x1, other arithmetic, shards(): masked = jnp.where(kept_mask[None, None], spectra, 0.0).astype(jnp.bfloat16)  7.67 us
    another operation x2, other arithmetic  7.03 us
    ppermute x1, starting transfers between devices, with_halo(): lax.ppermute(head, axis, [((i + 1) % count, i) for i in range(ends)])  6.94 us
  transfers between devices with their start and end apart: 3, of which 2 were waited for; matrix products, arithmetic and copies ran while one was open for 11% of the time, Pallas kernels for 0%

commit v1 on v0

v1 whole, which is shorter than its diff:
```python
import math

import jax
import jax.numpy as jnp
import numpy as np
from jax import lax
from jax.experimental import pallas as pl
from jax.experimental.pallas import tpu as pltpu
from jax.sharding import PartitionSpec as P

MESH = pl.DeviceIdType.MESH
BF16 = jnp.bfloat16
F32 = jnp.float32

LOWEST_ORDER = 512
NLAT = 1536
NLAT_W = 128
LONGITUDE_COUNT = 3072
HALF = LONGITUDE_COUNT // 2
RADIUS_IN = 0.35 / 0.65
ELSASSER = 0.5
SHELLS = 256

GX, NZ, NQ = 4, 8, 8
PEERS = GX * NQ
PAIRS = NZ // 2
WIDTH = 640


def lanes_of(zb):
    return 512 - 128 * (zb // 2)


def order_permutation():
    p = np.zeros((192, 192), np.float32)
    for x in range(GX):
        for v in range(3):
            for o in range(2):
                for k in range(PAIRS):
                    for part in range(2):
                        p[x * 48 + v * 16 + o * 8 + k * 2 + part, k * 48 + (2 * v + part) * 8 + 2 * x + o] = 1
    return p


def fourier_table():
    x, q, h, k = np.meshgrid(np.arange(GX), np.arange(NQ), np.arange(2), np.arange(PAIRS), indexing="ij")
    zb = np.where(h == 0, k, NZ - 1 - k)
    first = (64 * zb + 8 * q + 2 * x).reshape(-1)
    n = np.arange(HALF)
    out = np.zeros((2, first.size, 2, HALF), np.float32)
    for o in range(2):
        phase = ((LOWEST_ORDER + first + o)[:, None] * n[None, :]) % LONGITUDE_COUNT
        angle = phase * (2.0 * math.pi / LONGITUDE_COUNT)
        out[o, :, 0] = np.cos(angle)
        out[o, :, 1] = -np.sin(angle)
    return out.reshape(2, 2 * first.size, HALF)


def exchange_kernel(
    counts, spectra, legendre, perm, out,
    rows, packed, sends, recv, basis, fd, low, high,
    rows_sem, own_sem, spec_send, spec_recv, leg_send, leg_recv,
    end_send, end_recv, out_send, out_recv, local_sem,
):
    gx = lax.axis_index("grp")
    sub = lax.axis_index("sub")
    z, q = sub // NQ, sub % NQ
    me = gx * NQ + q
    up, down = (z + 1) % NZ, (z + NZ - 1) % NZ

    def peer(x, qq):
        return (x, z * NQ + qq)

    def along(zz):
        return (gx, zz * NQ + q)

    def row_copies(qq):
        return [
            pltpu.make_async_copy(
                spectra.at[0, :, pl.ds(64 * zb + 8 * qq, 8), pl.ds(0, lanes_of(zb))],
                rows.at[:, pl.ds(64 * zb + 8 * qq, 8), pl.ds(0, lanes_of(zb))],
                rows_sem.at[qq, zb],
            )
            for zb in range(NZ)
        ]

    @pl.loop(0, NQ)
    def _(i):
        for copy in row_copies((q + i) % NQ):
            copy.start()

    own = pltpu.make_async_copy(legendre.at[pl.ds(2 * gx, 2)], basis.at[z], own_sem)
    own.start()

    barrier = pltpu.get_barrier_semaphore()

    @pl.loop(0, PEERS)
    def _(i):
        @pl.when(i != me)
        def _():
            pl.semaphore_signal(barrier, inc=1, device_id=peer(i // NQ, i % NQ), device_id_type=MESH)

    for zz in (up, down):
        pl.semaphore_signal(barrier, inc=1, device_id=along(zz), device_id_type=MESH)

    limit = counts[gx, 0]

    def pack(qq):
        for copy in row_copies(qq):
            copy.wait()
        for k in range(PAIRS):
            parts = []
            for zb in (k, NZ - 1 - k):
                width = lanes_of(zb)
                block = rows[:, pl.ds(64 * zb + 8 * qq, 8), pl.ds(0, width)]
                order = lax.broadcasted_iota(jnp.int32, (8, width), 0) + (64 * zb + 8 * qq)
                degree = lax.broadcasted_iota(jnp.int32, (8, width), 1)
                keep = degree < jnp.maximum(limit - order, 1)
                block = jnp.where(keep[None], block, 0.0)
                parts.append(block.reshape(48, width))
            packed[pl.ds(48 * k, 48), :] = jnp.concatenate(parts, axis=1).astype(BF16)
        mixed = jnp.dot(perm[...], packed[...], preferred_element_type=F32)
        sends[qq] = mixed.astype(BF16).reshape(GX, 48, WIDTH)

    def spec_copy(x, qq):
        to = x * NQ + qq
        return pltpu.make_async_remote_copy(
            src_ref=sends.at[qq, x],
            dst_ref=recv.at[me],
            send_sem=spec_send.at[to],
            recv_sem=spec_recv.at[me],
            device_id=peer(x, qq),
            device_id_type=MESH,
        )

    def spec_arrival(frm):
        return pltpu.make_async_remote_copy(
            src_ref=sends.at[0, 0],
            dst_ref=recv.at[frm],
            send_sem=spec_send.at[frm],
            recv_sem=spec_recv.at[frm],
            device_id=peer(frm // NQ, frm % NQ),
            device_id_type=MESH,
        )

    def send_spec(qq):
        @pl.loop(0, GX)
        def _(j):
            x = (gx + j) % GX

            @pl.when(x * NQ + qq != me)
            def _():
                spec_copy(x, qq).start()

    def leg_copies(step, way):
        zb = (z + NZ - step) % NZ if way == 0 else (z + step) % NZ
        target = up if way == 0 else down
        orders = pl.ds(0, 2) if step < 3 else pl.ds(way, 1)
        result = []
        for t in range(4):
            lanes = pl.ds(128 * t, 128)
            if step == 0:
                src = legendre.at[pl.ds(2 * gx, 2), :, lanes]
            else:
                src = basis.at[zb, orders, :, lanes]
            copy = pltpu.make_async_remote_copy(
                src_ref=src,
                dst_ref=basis.at[zb, orders, :, lanes],
                send_sem=leg_send.at[way, step, t],
                recv_sem=leg_recv.at[way, step, t],
                device_id=along(target),
                device_id_type=MESH,
            )
            result.append((t < 4 - zb // 2, copy))
        return result

    def leg_arrivals(step, way):
        zb = (z + NZ - step - 1) % NZ if way == 0 else (z + step + 1) % NZ
        orders = pl.ds(0, 2) if step < 3 else pl.ds(way, 1)
        result = []
        for t in range(4):
            lanes = pl.ds(128 * t, 128)
            copy = pltpu.make_async_remote_copy(
                src_ref=basis.at[zb, orders, :, lanes],
                dst_ref=basis.at[zb, orders, :, lanes],
                send_sem=leg_send.at[way, step, t],
                recv_sem=leg_recv.at[way, step, t],
                device_id=along(down if way == 0 else up),
                device_id_type=MESH,
            )
            result.append((t < 4 - zb // 2, copy))
        return result

    def leg_start(step):
        for way in range(2):
            for here, copy in leg_copies(step, way):
                @pl.when(here)
                def _():
                    copy.start()

    def leg_wait(step):
        for way in range(2):
            for here, copy in leg_arrivals(step, way):
                @pl.when(here)
                def _():
                    copy.wait_recv()

    pack(q)
    pl.semaphore_wait(barrier, PEERS - 1 + 2)
    leg_start(0)
    send_spec(q)
    mine = pltpu.make_async_copy(sends.at[q, gx], recv.at[me], local_sem.at[0])
    mine.start()

    @pl.loop(1, 4)
    def _(i):
        pack((q + i) % NQ)
        send_spec((q + i) % NQ)

    leg_wait(0)
    leg_start(1)

    @pl.loop(4, NQ)
    def _(i):
        pack((q + i) % NQ)
        send_spec((q + i) % NQ)

    leg_wait(1)
    leg_start(2)
    leg_wait(2)
    leg_start(3)
    own.wait()
    mine.wait()
    leg_wait(3)

    def out_copy(x, qq, what):
        to = x * NQ + qq
        return pltpu.make_async_remote_copy(
            src_ref=fd.at[x, qq, what],
            dst_ref=out.at[what, :, :, me],
            send_sem=out_send.at[to],
            recv_sem=out_recv.at[me],
            device_id=peer(x, qq),
            device_id_type=MESH,
        )

    def end_copies(x):
        return [
            pltpu.make_async_remote_copy(
                src_ref=fd.at[x, NQ - 1, 0],
                dst_ref=low.at[x],
                send_sem=end_send.at[0, x],
                recv_sem=end_recv.at[0, x],
                device_id=along(up),
                device_id_type=MESH,
            ),
            pltpu.make_async_remote_copy(
                src_ref=fd.at[x, 0, 0],
                dst_ref=high.at[x],
                send_sem=end_send.at[1, x],
                recv_sem=end_recv.at[1, x],
                device_id=along(down),
                device_id_type=MESH,
            ),
        ]

    rows384 = lax.broadcasted_iota(jnp.int32, (384, 128), 0)
    odd = rows384 % 16 >= 8
    pair_of = rows384 % 8 // 2

    @pl.loop(0, GX)
    def _(j):
        x = (gx + j) % GX

        @pl.loop(0, NQ)
        def _(i):
            @pl.when(x * NQ + i != me)
            def _():
                spec_arrival(x * NQ + i).wait_recv()

        total = [jnp.zeros((384, 128), F32)] * 2
        for k in range(PAIRS):
            first = lanes_of(k)
            for h, zb in enumerate((k, NZ - 1 - k)):
                width = lanes_of(zb)
                left = recv[pl.ds(x * NQ, NQ), :, pl.ds(h * first, width)].reshape(384, width)
                right = basis[zb, :, :, pl.ds(0, width)].reshape(256, width)
                both = lax.dot_general(left, right, (((1,), (1,)), ((), ())), preferred_element_type=F32)
                one = jnp.where(odd, both[:, 128:], both[:, :128])
                total[h] = jnp.where(pair_of == k, one, total[h])
        fourier = jnp.concatenate([t.reshape(NQ, 3, 2, 8, 128) for t in total], axis=3).astype(BF16)
        fd[x, :, 0] = fourier
        for copy in end_copies(x):
            copy.start()
        wide = fourier.astype(F32)
        fd[x, 1 : NQ - 1, 1] = (0.5 * (wide[2:] - wide[:-2])).astype(BF16)

        @pl.loop(0, NQ)
        def _(i):
            qq = (q + i) % NQ
            inner = (qq > 0) & (qq < NQ - 1)

            @pl.when((x * NQ + qq != me) & inner)
            def _():
                out_copy(x, qq, pl.ds(0, 2)).start()

            @pl.when((x * NQ + qq != me) & jnp.logical_not(inner))
            def _():
                out_copy(x, qq, pl.ds(0, 1)).start()

    for x in range(GX):
        for copy in end_copies(x):
            copy.wait_recv()

    for x in range(GX):
        bottom = fd[x, 0, 0].astype(F32)
        second = fd[x, 1, 0].astype(F32)
        below = low[x].astype(F32)
        before = low[x - 1].astype(F32) if x > 0 else 2.0 * bottom - second
        below = jnp.where(z == 0, before, below)
        fd[x, 0, 1] = (0.5 * (second - below)).astype(BF16)
        top = fd[x, NQ - 1, 0].astype(F32)
        last = fd[x, NQ - 2, 0].astype(F32)
        above = high[x].astype(F32)
        after = high[x + 1].astype(F32) if x < GX - 1 else 2.0 * top - last
        above = jnp.where(z == NZ - 1, after, above)
        fd[x, NQ - 1, 1] = (0.5 * (above - last)).astype(BF16)
        for qq in (0, NQ - 1):
            @pl.when(x * NQ + qq != me)
            def _():
                out_copy(x, qq, pl.ds(1, 1)).start()

    keep = pltpu.make_async_copy(fd.at[gx, q], out.at[:, :, :, me], local_sem.at[1])
    keep.start()
    keep.wait()

    @pl.loop(0, PEERS)
    def _(i):
        @pl.when(i != me)
        def _():
            out_arrival = pltpu.make_async_remote_copy(
                src_ref=fd.at[i // NQ, i % NQ],
                dst_ref=out.at[:, :, :, i],
                send_sem=out_send.at[i],
                recv_sem=out_recv.at[i],
                device_id=peer(i // NQ, i % NQ),
                device_id_type=MESH,
            )
            out_arrival.wait_recv()
            out_arrival.wait_send()
            spec_copy(i // NQ, i % NQ).wait_send()

    for x in range(GX):
        for copy in end_copies(x):
            copy.wait_send()
    for step in range(4):
        for way in range(2):
            for here, copy in leg_copies(step, way):
                @pl.when(here)
                def _():
                    copy.wait_send()


def exchange(counts, spectra, legendre, perm):
    return pl.pallas_call(
        exchange_kernel,
        out_shape=jax.ShapeDtypeStruct((2, 3, 2, PEERS, 16, 128), BF16),
        in_specs=[
            pl.BlockSpec(memory_space=pltpu.SMEM),
            pl.BlockSpec(memory_space=pl.ANY),
            pl.BlockSpec(memory_space=pl.ANY),
            pl.BlockSpec(memory_space=pltpu.VMEM),
        ],
        out_specs=pl.BlockSpec(memory_space=pl.ANY),
        scratch_shapes=[
            pltpu.VMEM((6, 512, 512), F32),
            pltpu.VMEM((192, WIDTH), BF16),
            pltpu.VMEM((NQ, GX, 48, WIDTH), BF16),
            pltpu.VMEM((PEERS, 48, WIDTH), BF16),
            pltpu.VMEM((NZ, 2, 128, 512), BF16),
            pltpu.VMEM((GX, NQ, 2, 3, 2, 16, 128), BF16),
            pltpu.VMEM((GX, 3, 2, 16, 128), BF16),
            pltpu.VMEM((GX, 3, 2, 16, 128), BF16),
            pltpu.SemaphoreType.DMA((NQ, NZ)),
            pltpu.SemaphoreType.DMA,
            pltpu.SemaphoreType.DMA((PEERS,)),
            pltpu.SemaphoreType.DMA((PEERS,)),
            pltpu.SemaphoreType.DMA((2, 4, 4)),
            pltpu.SemaphoreType.DMA((2, 4, 4)),
            pltpu.SemaphoreType.DMA((2, GX)),
            pltpu.SemaphoreType.DMA((2, GX)),
            pltpu.SemaphoreType.DMA((PEERS,)),
            pltpu.SemaphoreType.DMA((PEERS,)),
            pltpu.SemaphoreType.DMA((2,)),
        ],
        compiler_params=pltpu.CompilerParams(
            collective_id=0, has_side_effects=True, vmem_limit_bytes=40 * 2**20
        ),
        cost_estimate=pl.CostEstimate(flops=2 * 10**9, bytes_accessed=10**7, transcendentals=0),
    )(counts, spectra, legendre, perm)


TILE = 256
STEPS = HALF // TILE


def synthesis_kernel(field, geometry, fd, table, out, left, later):
    half = pl.program_id(1)

    @pl.when((pl.program_id(0) == 0) & (half == 0))
    def _():
        for o in range(2):
            for what in range(2):
                for v in range(3):
                    block = fd[what, v, o].reshape(512, 128)
                    left[o, pl.ds(128 * (3 * what + v), 128), :] = block.T

    squared = field[0]
    cos_theta = geometry[:, 0:1]
    sin_theta = geometry[:, 1:2]

    def terms(flow):
        radial, polar, azimuth = flow[0:128], flow[128:256], flow[256:384]
        slope = [flow[384:512], flow[512:640], flow[640:768]]
        mix = squared * cos_theta * sin_theta
        out[0, 0] = (
            sin_theta * azimuth + mix * polar - radial * (0.5 * squared * sin_theta * sin_theta + slope[0])
        ).astype(BF16)
        out[0, 1] = (
            cos_theta * azimuth + mix * radial - 2.0 * squared * cos_theta * cos_theta * polar - radial * slope[1]
        ).astype(BF16)
        total = 0.5 * squared * (4.0 * cos_theta * cos_theta + sin_theta * sin_theta)
        out[0, 2] = (-cos_theta * polar - total * azimuth - radial * (sin_theta + slope[2])).astype(BF16)

    @pl.when(half == 0)
    def _():
        even = jnp.dot(left[0], table[0], preferred_element_type=F32)
        odd = jnp.dot(left[1], table[1], preferred_element_type=F32)
        later[...] = even - odd
        terms(even + odd)

    @pl.when(half == 1)
    def _():
        terms(later[...])


def synthesis(field, geometry, fd, table):
    return pl.pallas_call(
        synthesis_kernel,
        grid=(STEPS, 2),
        out_shape=jax.ShapeDtypeStruct((1, 3, NLAT_W, LONGITUDE_COUNT), BF16),
        in_specs=[
            pl.BlockSpec(memory_space=pltpu.SMEM),
            pl.BlockSpec((NLAT_W, 2), lambda i, h: (0, 0)),
            pl.BlockSpec((2, 3, 2, PEERS, 16, 128), lambda i, h: (0, 0, 0, 0, 0, 0)),
            pl.BlockSpec((2, 512, TILE), lambda i, h: (0, 0, i)),
        ],
        out_specs=pl.BlockSpec((1, 3, NLAT_W, TILE), lambda i, h: (0, 0, 0, h * STEPS + i)),
        scratch_shapes=[
            pltpu.VMEM((2, 768, 512), BF16),
            pltpu.VMEM((768, TILE), F32),
        ],
        compiler_params=pltpu.CompilerParams(vmem_limit_bytes=40 * 2**20),
        cost_estimate=pl.CostEstimate(flops=3 * 10**9, bytes_accessed=7 * 10**6, transcendentals=0),
    )(field, geometry, fd, table)


def shards(spectra, legendre, degree_counts):
    perm = jnp.asarray(order_permutation(), BF16)
    table = jnp.asarray(fourier_table(), BF16)
    theta = np.pi * (np.arange(NLAT_W) + (NLAT - NLAT_W) // 2 + 0.5) / NLAT
    geometry = jnp.asarray(np.stack([np.cos(theta), np.sin(theta)], axis=1), F32)
    shell = lax.axis_index(("grp", "sub")).astype(F32)
    radius = RADIUS_IN + (shell + 0.5) / SHELLS
    field = ((RADIUS_IN / radius) ** 6).reshape(1)
    fd = exchange(degree_counts, spectra, legendre, perm)
    return synthesis(field, geometry, fd, table)


def solution(mesh):
    in_specs = (P(("grp", "sub"), None, None, None), P("sub", None, None), P())
    out_specs = P(("grp", "sub"), None, None, None)
    return jax.shard_map(shards, mesh=mesh, in_specs=in_specs, out_specs=out_specs, check_vma=False)
```

time: 249 us -> 84.4 us (0.34)
  blocking collectives: 108 us -> 0 us
  Pallas kernels: 0 us -> 78.5 us
  waiting for transfers between devices: 57.8 us -> 0 us
  other arithmetic: 51.5 us -> 0 us
  matrix products: 14.4 us -> 0 us
  starting transfers between devices: 14.4 us -> 0 us
  local copies, waits for them, and re-layouts: 2.32 us -> 5.6 us
    all_to_all x1 -> x0, blocking collectives: 108 us -> none  [shards(): lax.all_to_all(masked, 'sub', split_axis=2, concat_axis=0, tiled=True)]
    pallas_call x0 -> x2, Pallas kernels: none -> 78.5 us  [the longest x1 70 us: exchange(): pl.pallas_call(exchange_kernel, out_shape=jax.ShapeDtypeStruct((2, 3, 2,...]
    ppermute x2 -> x0, waiting for transfers between devices: 57.8 us -> none  [the longest x1 49.7 us: with_halo(): lax.ppermute(head, axis, [((i + 1) % count, i) for i in range(ends)])]
    cos x2 -> x0, other arithmetic: 28.1 us -> none  [the longest x1 28 us: shards(): synth_table = jnp.stack([jnp.cos(angles), -jnp.sin(angles)])]
    dot_general x2 -> x0, matrix products: 14.4 us -> none  [the longest x1 10.8 us: shards(): jnp.einsum('mrcql,qmp->rclp', grouped, synth_table, precision=lax.Precisi...]
    ppermute x2 -> x0, starting transfers between devices: 8.86 us -> none  [the longest x1 6.94 us: with_halo(): lax.ppermute(head, axis, [((i + 1) % count, i) for i in range(ends)])]
    another operation x3 -> x0, other arithmetic: 8.69 us -> none
    convert_element_type x1 -> x0, other arithmetic: 7.67 us -> none  [shards(): masked = jnp.where(kept_mask[None, None], spectra, 0.0).astype(jnp.bfloat16)]
  transfers between devices with their start and end apart: 3 -> 0, of which waited for: 2 -> 0; matrix products, arithmetic and copies ran while one was open for 11% -> 0% of each run, Pallas kernels for 0% -> 0%
where the time goes in v1:
time: 84.4 us; the launch traced here: 84.2 us
  Pallas kernels  78.5 us (93%)
  local copies, waits for them, and re-layouts  5.6 us (7%)
    pallas_call x1, Pallas kernels, exchange(): pl.pallas_call(exchange_kernel, out_shape=jax.ShapeDtypeStruct((2, 3, 2,...  70 us
    pallas_call x1, Pallas kernels, synthesis(): pl.pallas_call(synthesis_kernel, grid=(STEPS, 2), out_shape=jax.ShapeDtyp...  8.56 us
    unnamed x12, local copies, waits for them, and re-layouts  5.6 us

profile of v1, /device:TPU:6, one launch (start us, length us, event | category | flops | bytes accessed | tf_op | source)
XLA Modules:
  0.0 84.2 jit_solution(11629667653869016763)
XLA Ops:
  0.1 0.0 copy-start
  0.1 2.8 %copy-done = f32[1,6,512,512]{3,2,1,0:T(8,128)S(1)} copy-done((f32[1,6,512,512]{3,2,1,0:T(8,128)S(1)}, f32[1,6,512,512]{3,2,1,0:T(8,128)}, u32[]{:S(2)}) %copy-start) | copy-done | bytes 6291480
  2.8 0.0 copy-start.1
  2.8 1.2 %copy-done.1 = bf16[8,128,512]{2,1,0:T(8,128)(2,1)S(1)} copy-done((bf16[8,128,512]{2,1,0:T(8,128)(2,1)S(1)}, bf16[8,128,512]{2,1,0:T(8,128)(2,1)}, u32[]{:S(2)}) %copy-start.1) | copy-done | bytes 1048600
  4.1 0.0 copy-start.2
  4.1 0.9 %copy-done.2 = bf16[192,192]{1,0:T(8,128)(2,1)S(1)} copy-done((bf16[192,192]{1,0:T(8,128)(2,1)S(1)}, bf16[192,192]{1,0:T(8,128)(2,1)}, u32[]{:S(2)}) %copy-start.2) | copy-done | bytes 73752
  5.0 0.0 copy-start.3
  5.0 0.7 copy-done.3
  5.7 0.0 copy-start.4
  5.7 0.0 copy-start.5
  5.7 70.0 %shard_map.64.fd = bf16[2,3,2,32,16,128]{5,4,3,2,1,0:T(8,128)(2,1)S(1)} custom-call(s32[4,512]{1,0:T(4,128)S(1)} %copy-done.3, f32[1,6,512,512]{3,2,1,0:T(8,128)S(1)} %copy-done, bf16[8,128,512]{2,1,0:T(8,128)(2,1)S(1)} %copy-done.1, bf16[192,192]{1,0:T(8,128)(2,1)S(1)} %copy-done.2), custom_call_target="tpu_custom_call" | custom-call | flops 2000000000 | bytes 10000000 | tf_op jit(solution)/shard_map/pallas_call | solution.py:365
  75.6 0.0 copy-done.4
  75.6 0.0 copy-done.5
  75.7 8.6 %shard_map.65 = bf16[1,3,128,3072]{3,2,1,0:T(8,128)(2,1)} custom-call(f32[1]{0:T(128)} %bitcast.field, f32[128,2]{1,0:T(8,128)S(1)} %copy-done.5, bf16[2,3,2,32,16,128]{5,4,3,2,1,0:T(8,128)(2,1)S(1)} %shard_map.64.fd, bf16[2,512,1536]{2,1,0:T(8,128)(2,1)S(1)} %copy-done.4), custom_call_target="tpu_custom_call" | custom-call | flops 3000000000 | bytes 7000000 | tf_op jit(solution)/shard_map/pallas_call | solution.py:448
Async XLA Ops:
  0.1 2.8 %copy-start = (f32[1,6,512,512]{3,2,1,0:T(8,128)S(1)}, f32[1,6,512,512]{3,2,1,0:T(8,128)}, u32[]{:S(2)}) copy-start(f32[1,6,512,512]{3,2,1,0:T(8,128)} %spectra.1) | copy-start | bytes 18874372
  2.8 1.2 %copy-start.1 = (bf16[8,128,512]{2,1,0:T(8,128)(2,1)S(1)}, bf16[8,128,512]{2,1,0:T(8,128)(2,1)}, u32[]{:S(2)}) copy-start(bf16[8,128,512]{2,1,0:T(8,128)(2,1)} %legendre.1) | copy-start | bytes 3145732
  4.1 0.9 %copy-start.2 = (bf16[192,192]{1,0:T(8,128)(2,1)S(1)}, bf16[192,192]{1,0:T(8,128)(2,1)}, u32[]{:S(2)}) copy-start(bf16[192,192]{1,0:T(8,128)(2,1)} %constant.24.clone.perm) | copy-start | bytes 221188
  5.0 0.7 copy-start.3
  5.7 70.0 %copy-start.4 = (bf16[2,512,1536]{2,1,0:T(8,128)(2,1)S(1)}, bf16[2,512,1536]{2,1,0:T(8,128)(2,1)}, u32[]{:S(2)}) copy-start(bf16[2,512,1536]{2,1,0:T(8,128)(2,1)} %constant.25.clone.table) | copy-start | bytes 9437188
  5.7 70.0 %copy-start.5 = (f32[128,2]{1,0:T(8,128)S(1)}, f32[128,2]{1,0:T(8,128)}, u32[]{:S(2)}) copy-start(f32[128,2]{1,0:T(8,128)} %constant.26.clone.geometry) | copy-start | bytes 3076

commit v2 on v1

v2 whole, which is shorter than its diff:
```python
import math

import jax
import jax.numpy as jnp
import numpy as np
from jax import lax
from jax.experimental import pallas as pl
from jax.experimental.pallas import tpu as pltpu
from jax.sharding import PartitionSpec as P

MESH = pl.DeviceIdType.MESH
BF16 = jnp.bfloat16
F32 = jnp.float32

LOWEST_ORDER = 512
NLAT = 1536
NLAT_W = 128
LONGITUDE_COUNT = 3072
HALF = LONGITUDE_COUNT // 2
RADIUS_IN = 0.35 / 0.65
ELSASSER = 0.5
SHELLS = 256

GX, NZ, NQ = 4, 8, 8
PEERS = GX * NQ
PAIRS = NZ // 2
WIDTH = 640


def lanes_of(zb):
    return 512 - 128 * (zb // 2)


def order_permutation():
    p = np.zeros((192, 192), np.float32)
    for x in range(GX):
        for v in range(3):
            for o in range(2):
                for k in range(PAIRS):
                    for part in range(2):
                        p[x * 48 + v * 16 + o * 8 + k * 2 + part, k * 48 + (2 * v + part) * 8 + 2 * x + o] = 1
    return p


def fourier_table():
    x, q, h, k = np.meshgrid(np.arange(GX), np.arange(NQ), np.arange(2), np.arange(PAIRS), indexing="ij")
    zb = np.where(h == 0, k, NZ - 1 - k)
    first = (64 * zb + 8 * q + 2 * x).reshape(-1)
    n = np.arange(HALF)
    out = np.zeros((2, first.size, 2, HALF), np.float32)
    for o in range(2):
        phase = ((LOWEST_ORDER + first + o)[:, None] * n[None, :]) % LONGITUDE_COUNT
        angle = phase * (2.0 * math.pi / LONGITUDE_COUNT)
        out[o, :, 0] = np.cos(angle)
        out[o, :, 1] = -np.sin(angle)
    return out.reshape(2, 2 * first.size, HALF)


def exchange_kernel(
    counts, spectra, legendre, perm, left,
    limits, mixer, rows, packed, sends, recv, basis, fd, low, high, field,
    limit_sem, mixer_sem, rows_sem, own_sem, spec_send, spec_recv, leg_send, leg_recv,
    end_send, end_recv, out_send, out_recv, local_sem,
):
    gx = lax.axis_index("grp")
    sub = lax.axis_index("sub")
    z, q = sub // NQ, sub % NQ
    me = gx * NQ + q
    up, down = (z + 1) % NZ, (z + NZ - 1) % NZ

    def peer(x, qq):
        return (x, z * NQ + qq)

    def along(zz):
        return (gx, zz * NQ + q)

    barrier = pltpu.get_barrier_semaphore()

    @pl.loop(0, PEERS)
    def _(i):
        @pl.when(i != me)
        def _():
            pl.semaphore_signal(barrier, inc=1, device_id=peer(i // NQ, i % NQ), device_id_type=MESH)

    for zz in (up, down):
        pl.semaphore_signal(barrier, inc=1, device_id=along(zz), device_id_type=MESH)

    limit_copy = pltpu.make_async_copy(counts, limits, limit_sem)
    limit_copy.start()
    mixer_copy = pltpu.make_async_copy(perm, mixer, mixer_sem)
    mixer_copy.start()

    def row_copies(qq):
        return [
            pltpu.make_async_copy(
                spectra.at[0, :, pl.ds(64 * zb + 8 * qq, 8), pl.ds(0, lanes_of(zb))],
                rows.at[:, pl.ds(64 * zb + 8 * qq, 8), pl.ds(0, lanes_of(zb))],
                rows_sem.at[qq, zb],
            )
            for zb in range(NZ)
        ]

    @pl.loop(0, NQ)
    def _(i):
        for copy in row_copies((q + i) % NQ):
            copy.start()

    own = pltpu.make_async_copy(legendre.at[pl.ds(2 * gx, 2)], basis.at[z], own_sem)
    own.start()

    def pack(qq):
        for copy in row_copies(qq):
            copy.wait()
        limit = limits[gx, 0]
        for k in range(PAIRS):
            parts = []
            for zb in (k, NZ - 1 - k):
                width = lanes_of(zb)
                block = rows[:, pl.ds(64 * zb + 8 * qq, 8), pl.ds(0, width)]
                order = lax.broadcasted_iota(jnp.int32, (8, width), 0) + (64 * zb + 8 * qq)
                degree = lax.broadcasted_iota(jnp.int32, (8, width), 1)
                keep = degree < jnp.maximum(limit - order, 1)
                block = jnp.where(keep[None], block, 0.0)
                parts.append(block.reshape(48, width))
            packed[pl.ds(48 * k, 48), :] = jnp.concatenate(parts, axis=1).astype(BF16)
        mixed = jnp.dot(mixer[...], packed[...], preferred_element_type=F32)
        sends[qq] = mixed.astype(BF16).reshape(GX, 48, WIDTH)

    def spec_copy(x, qq):
        return pltpu.make_async_remote_copy(
            src_ref=sends.at[qq, x],
            dst_ref=recv.at[q, gx],
            send_sem=spec_send.at[qq, x],
            recv_sem=spec_recv.at[q, gx],
            device_id=peer(x, qq),
            device_id_type=MESH,
        )

    def spec_arrival(x, qq):
        return pltpu.make_async_remote_copy(
            src_ref=sends.at[qq, x],
            dst_ref=recv.at[qq, x],
            send_sem=spec_send.at[qq, x],
            recv_sem=spec_recv.at[qq, x],
            device_id=peer(x, qq),
            device_id_type=MESH,
        )

    def send_spec(qq):
        @pl.loop(0, GX)
        def _(j):
            x = (gx + j) % GX

            @pl.when(x * NQ + qq != me)
            def _():
                spec_copy(x, qq).start()

    def leg_piece(step, way, t, arriving):
        shift = step + 1 if arriving else step
        zb = (z + NZ - shift) % NZ if way == 0 else (z + shift) % NZ
        onward = (up, down)[way]
        backward = (down, up)[way]
        orders = pl.ds(0, 2) if step < 3 else pl.ds(way, 1)
        lanes = pl.ds(128 * t, 128)
        src = basis.at[zb, orders, :, lanes]
        if step == 0 and not arriving:
            src = legendre.at[pl.ds(2 * gx, 2), :, lanes]
        copy = pltpu.make_async_remote_copy(
            src_ref=src,
            dst_ref=basis.at[zb, orders, :, lanes],
            send_sem=leg_send.at[way, step, t],
            recv_sem=leg_recv.at[way, step, t],
            device_id=along(backward if arriving else onward),
            device_id_type=MESH,
        )
        return t < 4 - zb // 2, copy

    def leg_first():
        for t in range(4):
            for way in range(2):
                here, copy = leg_piece(0, way, t, False)
                pl.when(here)(copy.start)

    def leg_forward(step):
        for t in range(4):
            for way in range(2):
                here, arrival = leg_piece(step, way, t, True)

                @pl.when(here)
                def _():
                    arrival.wait_recv()
                    if step < 3:
                        leg_piece(step + 1, way, t, False)[1].start()

    limit_copy.wait()
    mixer_copy.wait()
    pack(q)
    pl.semaphore_wait(barrier, PEERS - 1 + 2)
    leg_first()
    send_spec(q)
    mine = pltpu.make_async_copy(sends.at[q, gx], recv.at[q, gx], local_sem.at[0])
    mine.start()

    def pack_and_send(i):
        pack((q + i) % NQ)
        send_spec((q + i) % NQ)

    pl.loop(1, 4)(pack_and_send)
    leg_forward(0)
    pl.loop(4, 6)(pack_and_send)
    leg_forward(1)
    pl.loop(6, 8)(pack_and_send)
    leg_forward(2)
    leg_forward(3)
    own.wait()
    mine.wait()

    def out_copy(x, qq, what):
        return pltpu.make_async_remote_copy(
            src_ref=fd.at[qq, x, what],
            dst_ref=field.at[what, :, :, me],
            send_sem=out_send.at[what, qq, x],
            recv_sem=out_recv.at[what, q, gx],
            device_id=peer(x, qq),
            device_id_type=MESH,
        )

    def out_arrival(x, qq, what):
        return pltpu.make_async_remote_copy(
            src_ref=fd.at[qq, x, what],
            dst_ref=field.at[what, :, :, x * NQ + qq],
            send_sem=out_send.at[what, qq, x],
            recv_sem=out_recv.at[what, qq, x],
            device_id=peer(x, qq),
            device_id_type=MESH,
        )

    def send_out(qq, what):
        @pl.loop(0, GX)
        def _(j):
            x = (gx + j) % GX

            @pl.when(x * NQ + qq != me)
            def _():
                out_copy(x, qq, what).start()

    def low_copy():
        return pltpu.make_async_remote_copy(
            src_ref=fd.at[NQ - 1, :, 0],
            dst_ref=low,
            send_sem=end_send.at[0],
            recv_sem=end_recv.at[0],
            device_id=along(up),
            device_id_type=MESH,
        )

    def high_copy():
        return pltpu.make_async_remote_copy(
            src_ref=fd.at[0, :, 0],
            dst_ref=high,
            send_sem=end_send.at[1],
            recv_sem=end_recv.at[1],
            device_id=along(down),
            device_id_type=MESH,
        )

    rows192 = lax.broadcasted_iota(jnp.int32, (192, 128), 0)
    odd = rows192 % 16 >= 8
    pair_of = rows192 % 8 // 2

    def inner_difference(m):
        @pl.when((m > 0) & (m < NQ - 1))
        def _():
            outer = fd[m + 1, :, 0].astype(F32)
            inner = fd[m - 1, :, 0].astype(F32)
            fd[m, :, 1] = (0.5 * (outer - inner)).astype(BF16)
            send_out(m, 1)

    @pl.loop(0, NQ)
    def _(i):
        qq = (q + NQ - i) % NQ

        @pl.loop(0, GX)
        def _(x):
            @pl.when(x * NQ + qq != me)
            def _():
                spec_arrival(x, qq).wait_recv()

        total = [jnp.zeros((192, 128), F32)] * 2
        for k in range(PAIRS):
            first = lanes_of(k)
            for h, zb in enumerate((k, NZ - 1 - k)):
                width = lanes_of(zb)
                block = recv[qq, :, :, pl.ds(h * first, width)].reshape(192, width)
                right = basis[zb, :, :, pl.ds(0, width)].reshape(256, width)
                both = lax.dot_general(block, right, (((1,), (1,)), ((), ())), preferred_element_type=F32)
                one = jnp.where(odd, both[:, 128:], both[:, :128])
                total[h] = jnp.where(pair_of == k, one, total[h])
        fourier = jnp.concatenate([t.reshape(GX, 3, 2, 8, 128) for t in total], axis=3).astype(BF16)
        fd[qq, :, 0] = fourier
        send_out(qq, 0)

        @pl.when(qq == NQ - 1)
        def _():
            low_copy().start()

        @pl.when(qq == 0)
        def _():
            high_copy().start()

        @pl.when(i >= 2)
        def _():
            inner_difference((qq + 1) % NQ)

    inner_difference((q + 1) % NQ)
    inner_difference(q)
    low_copy().wait_recv()
    high_copy().wait_recv()

    for x in range(GX):
        bottom = fd[0, x, 0].astype(F32)
        second = fd[1, x, 0].astype(F32)
        before = low[x - 1].astype(F32) if x > 0 else 2.0 * bottom - second
        below = jnp.where(z == 0, before, low[x].astype(F32))
        fd[0, x, 1] = (0.5 * (second - below)).astype(BF16)
        top = fd[NQ - 1, x, 0].astype(F32)
        last = fd[NQ - 2, x, 0].astype(F32)
        after = high[x + 1].astype(F32) if x < GX - 1 else 2.0 * top - last
        above = jnp.where(z == NZ - 1, after, high[x].astype(F32))
        fd[NQ - 1, x, 1] = (0.5 * (above - last)).astype(BF16)
    send_out(0, 1)
    send_out(NQ - 1, 1)

    keep = pltpu.make_async_copy(fd.at[q, gx], field.at[:, :, :, me], local_sem.at[1])
    keep.start()
    keep.wait()

    for what in range(2):
        @pl.loop(0, PEERS)
        def _(i):
            @pl.when(i != me)
            def _():
                out_arrival(i // NQ, i % NQ, what).wait_recv()

        for o in range(2):
            for v in range(3):
                block = field[what, v, o].reshape(512, 128)
                left[o, pl.ds(128 * (3 * what + v), 128), :] = block.T

    @pl.loop(0, PEERS)
    def _(i):
        @pl.when(i != me)
        def _():
            x, qq = i // NQ, i % NQ
            out_copy(x, qq, 0).wait_send()
            out_copy(x, qq, 1).wait_send()
            spec_copy(x, qq).wait_send()

    low_copy().wait_send()
    high_copy().wait_send()
    for step in range(4):
        for t in range(4):
            for way in range(2):
                here, copy = leg_piece(step, way, t, False)
                pl.when(here)(copy.wait_send)


def exchange(counts, spectra, legendre, perm):
    return pl.pallas_call(
        exchange_kernel,
        out_shape=jax.ShapeDtypeStruct((2, 768, 512), BF16),
        in_specs=[pl.BlockSpec(memory_space=pl.ANY)] * 4,
        out_specs=pl.BlockSpec(memory_space=pltpu.VMEM),
        scratch_shapes=[
            pltpu.SMEM((GX, 512), jnp.int32),
            pltpu.VMEM((192, 192), BF16),
            pltpu.VMEM((6, 512, 512), F32),
            pltpu.VMEM((192, WIDTH), BF16),
            pltpu.VMEM((NQ, GX, 48, WIDTH), BF16),
            pltpu.VMEM((NQ, GX, 48, WIDTH), BF16),
            pltpu.VMEM((NZ, 2, 128, 512), BF16),
            pltpu.VMEM((NQ, GX, 2, 3, 2, 16, 128), BF16),
            pltpu.VMEM((GX, 3, 2, 16, 128), BF16),
            pltpu.VMEM((GX, 3, 2, 16, 128), BF16),
            pltpu.VMEM((2, 3, 2, PEERS, 16, 128), BF16),
            pltpu.SemaphoreType.DMA,
            pltpu.SemaphoreType.DMA,
            pltpu.SemaphoreType.DMA((NQ, NZ)),
            pltpu.SemaphoreType.DMA,
            pltpu.SemaphoreType.DMA((NQ, GX)),
            pltpu.SemaphoreType.DMA((NQ, GX)),
            pltpu.SemaphoreType.DMA((2, 4, 4)),
            pltpu.SemaphoreType.DMA((2, 4, 4)),
            pltpu.SemaphoreType.DMA((2,)),
            pltpu.SemaphoreType.DMA((2,)),
            pltpu.SemaphoreType.DMA((2, NQ, GX)),
            pltpu.SemaphoreType.DMA((2, NQ, GX)),
            pltpu.SemaphoreType.DMA((2,)),
        ],
        compiler_params=pltpu.CompilerParams(
            collective_id=0, has_side_effects=True, vmem_limit_bytes=57 * 2**20
        ),
        cost_estimate=pl.CostEstimate(flops=2 * 10**9, bytes_accessed=10**7, transcendentals=0),
    )(counts, spectra, legendre, perm)


TILE = 256
STEPS = HALF // TILE
CHUNK = 16


def synthesis_kernel(field, geometry, left, table, out, factors, waves, stage, sems):
    squared = field[0]
    cos_theta = geometry[0]
    sin_theta = geometry[1]
    factors[0] = cos_theta
    factors[1] = sin_theta
    factors[2] = squared * cos_theta * sin_theta
    factors[3] = 0.5 * squared * sin_theta * sin_theta
    factors[4] = 2.0 * squared * cos_theta * cos_theta
    factors[5] = 0.5 * squared * (4.0 * cos_theta * cos_theta + sin_theta * sin_theta)

    def ship(i, h):
        return pltpu.make_async_copy(
            stage.at[i, h],
            out.at[0, :, :, pl.ds(h * HALF + i * TILE, TILE)],
            sems.at[i, h],
        )

    def wide(value):
        return jnp.concatenate([value] * (TILE // 128), axis=1)

    for i in range(STEPS):
        columns = pl.ds(i * TILE, TILE)
        for o in range(2):
            waves[i % 2, o] = jnp.dot(left[o], table[o, :, columns], preferred_element_type=F32)
        for r in range(0, NLAT_W, CHUNK):
            here = pl.ds(r, CHUNK)
            cos_w, sin_w, mix, own, twice, total = (wide(factors[n, here, :]) for n in range(6))
            even = [waves[i % 2, 0, pl.ds(128 * n + r, CHUNK), :] for n in range(6)]
            odd = [waves[i % 2, 1, pl.ds(128 * n + r, CHUNK), :] for n in range(6)]
            for h in range(2):
                flow = [a + b if h == 0 else a - b for a, b in zip(even, odd)]
                radial, polar, azimuth = flow[:3]
                stage[i, h, 0, here, :] = (
                    sin_w * azimuth + mix * polar - radial * (own + flow[3])
                ).astype(BF16)
                stage[i, h, 1, here, :] = (
                    cos_w * azimuth - twice * polar + radial * (mix - flow[4])
                ).astype(BF16)
                stage[i, h, 2, here, :] = (
                    -(cos_w * polar + total * azimuth + radial * (sin_w + flow[5]))
                ).astype(BF16)
        for h in range(2):
            ship(i, h).start()
    for i in range(STEPS):
        for h in range(2):
            ship(i, h).wait()


def synthesis(field, geometry, left, table):
    return pl.pallas_call(
        synthesis_kernel,
        out_shape=jax.ShapeDtypeStruct((1, 3, NLAT_W, LONGITUDE_COUNT), BF16),
        in_specs=[
            pl.BlockSpec(memory_space=pltpu.SMEM),
            pl.BlockSpec(memory_space=pltpu.VMEM),
            pl.BlockSpec(memory_space=pltpu.VMEM),
            pl.BlockSpec(memory_space=pltpu.VMEM),
        ],
        out_specs=pl.BlockSpec(memory_space=pl.ANY),
        scratch_shapes=[
            pltpu.VMEM((6, NLAT_W, 128), F32),
            pltpu.VMEM((2, 2, 768, TILE), F32),
            pltpu.VMEM((STEPS, 2, 3, NLAT_W, TILE), BF16),
            pltpu.SemaphoreType.DMA((STEPS, 2)),
        ],
        compiler_params=pltpu.CompilerParams(vmem_limit_bytes=32 * 2**20),
        cost_estimate=pl.CostEstimate(flops=3 * 10**9, bytes_accessed=7 * 10**6, transcendentals=0),
    )(field, geometry, left, table)


def shards(spectra, legendre, degree_counts):
    perm = jnp.asarray(order_permutation(), BF16)
    table = jnp.asarray(fourier_table(), BF16)
    theta = np.pi * (np.arange(NLAT_W) + (NLAT - NLAT_W) // 2 + 0.5) / NLAT
    geometry = np.repeat(np.stack([np.cos(theta), np.sin(theta)])[:, :, None], 128, axis=2)
    geometry = jnp.asarray(geometry, F32)
    shell = lax.axis_index(("grp", "sub")).astype(F32)
    radius = RADIUS_IN + (shell + 0.5) / SHELLS
    field = ((RADIUS_IN / radius) ** 6).reshape(1)
    left = exchange(degree_counts, spectra, legendre, perm)
    return synthesis(field, geometry, left, table)


def solution(mesh):
    in_specs = (P(("grp", "sub"), None, None, None), P("sub", None, None), P())
    out_specs = P(("grp", "sub"), None, None, None)
    return jax.shard_map(shards, mesh=mesh, in_specs=in_specs, out_specs=out_specs, check_vma=False)
```

time: 84.4 us -> 71.1 us (0.84)
  the two profiles are of different devices: /device:TPU:6 before, /device:TPU:249 now
where the time goes in v2:
time: 71.1 us; the launch traced here: 71 us
  Pallas kernels  69.5 us (98%)
  local copies, waits for them, and re-layouts  1.41 us (2%)
    pallas_call x1, Pallas kernels, exchange(): pl.pallas_call(exchange_kernel, out_shape=jax.ShapeDtypeStruct((2, 768, 5...  65.7 us
    pallas_call x1, Pallas kernels, synthesis(): pl.pallas_call(synthesis_kernel, out_shape=jax.ShapeDtypeStruct((1, 3, NL...  3.84 us

profile of v2, /device:TPU:249, one launch (start us, length us, event | category | flops | bytes accessed | tf_op | source)
XLA Modules:
  0.0 71.0 jit_solution(5858809569962533990)
XLA Ops:
  0.1 0.0 copy-start.1
  0.1 0.0 copy-start.2
  0.1 65.7 %shard_map.64.left = bf16[2,768,512]{2,1,0:T(8,128)(2,1)} custom-call(s32[4,512]{1,0:T(4,128)} %counts.1, f32[1,6,512,512]{3,2,1,0:T(8,128)} %spectra.1, bf16[8,128,512]{2,1,0:T(8,128)(2,1)} %legendre.1, bf16[192,192]{1,0:T(8,128)(2,1)} %constant.24.clone.perm), custom_call_target="tpu_custom_call" | custom-call | flops 2000000000 | bytes 10000000 | tf_op jit(solution)/shard_map/pallas_call | solution.py:369
  65.8 0.0 copy-done.1
  65.8 0.0 copy-done.2
  65.8 0.0 copy-start
  65.8 1.4 %copy-done = bf16[2,768,512]{2,1,0:T(8,128)(2,1)S(1)} copy-done((bf16[2,768,512]{2,1,0:T(8,128)(2,1)S(1)}, bf16[2,768,512]{2,1,0:T(8,128)(2,1)}, u32[]{:S(2)}) %copy-start) | copy-done | bytes 1572888
  67.2 3.8 %shard_map.65 = bf16[1,3,128,3072]{3,2,1,0:T(8,128)(2,1)} custom-call(f32[1]{0:T(128)} %bitcast.field, f32[2,128,128]{2,1,0:T(8,128)S(1)} %copy-done.2, bf16[2,768,512]{2,1,0:T(8,128)(2,1)S(1)} %copy-done, bf16[2,512,1536]{2,1,0:T(8,128)(2,1)S(1)} %copy-done.1), custom_call_target="tpu_custom_call" | custom-call | flops 3000000000 | bytes 7000000 | tf_op jit(solution)/shard_map/pallas_call | solution.py:462
Async XLA Ops:
  0.1 65.7 %copy-start.1 = (bf16[2,512,1536]{2,1,0:T(8,128)(2,1)S(1)}, bf16[2,512,1536]{2,1,0:T(8,128)(2,1)}, u32[]{:S(2)}) copy-start(bf16[2,512,1536]{2,1,0:T(8,128)(2,1)} %constant.25.clone.table) | copy-start | bytes 9437188
  0.1 65.7 %copy-start.2 = (f32[2,128,128]{2,1,0:T(8,128)S(1)}, f32[2,128,128]{2,1,0:T(8,128)}, u32[]{:S(2)}) copy-start(f32[2,128,128]{2,1,0:T(8,128)} %constant.26.clone.geometry) | copy-start | bytes 393220
  65.8 1.4 %copy-start = (bf16[2,768,512]{2,1,0:T(8,128)(2,1)S(1)}, bf16[2,768,512]{2,1,0:T(8,128)(2,1)}, u32[]{:S(2)}) copy-start(bf16[2,768,512]{2,1,0:T(8,128)(2,1)} %shard_map.64.left) | copy-start | bytes 4718596

commit v3 on v2

v3 whole, which is shorter than its diff:
```python
import math

import jax
import jax.numpy as jnp
import numpy as np
from jax import lax
from jax.experimental import pallas as pl
from jax.experimental.pallas import tpu as pltpu
from jax.sharding import PartitionSpec as P

MESH = pl.DeviceIdType.MESH
BF16 = jnp.bfloat16
F32 = jnp.float32

LOWEST_ORDER = 512
NLAT = 1536
NLAT_W = 128
LONGITUDE_COUNT = 3072
HALF = LONGITUDE_COUNT // 2
RADIUS_IN = 0.35 / 0.65
ELSASSER = 0.5
SHELLS = 256

GX, NZ, NQ = 4, 8, 8
PEERS = GX * NQ
PAIRS = NZ // 2
DEGREES = 512


def lanes_of(zb):
    return 512 - 128 * (zb // 2)


def order_permutation():
    p = np.zeros((192, 192), np.float32)
    for x in range(GX):
        for v in range(3):
            for o in range(2):
                for k in range(PAIRS):
                    for part in range(2):
                        p[x * 48 + v * 16 + o * 8 + k * 2 + part, k * 48 + (2 * v + part) * 8 + 2 * x + o] = 1
    return p


def fourier_table():
    x, q, h, k = np.meshgrid(np.arange(GX), np.arange(NQ), np.arange(2), np.arange(PAIRS), indexing="ij")
    block = 8 * k + q
    block = np.where(h == 0, block, np.where(block == 0, 32, 64 - block))
    first = (8 * block + 2 * x).reshape(-1)
    n = np.arange(HALF)
    out = np.zeros((2, first.size, 2, HALF), np.float32)
    for o in range(2):
        phase = ((LOWEST_ORDER + first + o)[:, None] * n[None, :]) % LONGITUDE_COUNT
        angle = phase * (2.0 * math.pi / LONGITUDE_COUNT)
        out[o, :, 0] = np.cos(angle)
        out[o, :, 1] = -np.sin(angle)
    return out.reshape(2, 2 * first.size, HALF)


def exchange_kernel(
    counts, spectra, legendre, perm, left,
    limits, mixer, rows, packed, sends, recv, sends_x, recv_x, basis, weights, weights_x, fd, low, high, field, turned,
    limit_sem, mixer_sem, rows_sem, own_send, own_recv, spec_send, spec_recv, x_send, x_recv, leg_send, leg_recv,
    end_send, end_recv, out_send, out_recv, left_sem,
):
    gx = lax.axis_index("grp")
    sub = lax.axis_index("sub")
    z, q = sub // NQ, sub % NQ
    me = gx * NQ + q
    y = q // 2
    up, down = (z + 1) % NZ, (z + NZ - 1) % NZ
    mirror = (NQ - q) % NQ
    column = jnp.where(z < PAIRS, q, mirror)

    def peer(x, qq):
        return (x, z * NQ + qq)

    def along(zz, qq):
        return (gx, zz * NQ + qq)

    barrier = pltpu.get_barrier_semaphore()

    @pl.loop(0, PEERS)
    def _(i):
        @pl.when(i != me)
        def _():
            pl.semaphore_signal(barrier, inc=1, device_id=peer(i // NQ, i % NQ), device_id_type=MESH)

    for zz in (up, down):
        for qq in (q, mirror):
            pl.semaphore_signal(barrier, inc=1, device_id=along(zz, qq), device_id_type=MESH)

    limit_copy = pltpu.make_async_copy(counts, limits, limit_sem)
    limit_copy.start()
    mixer_copy = pltpu.make_async_copy(perm, mixer, mixer_sem)
    mixer_copy.start()

    def pair_rows(k, qq):
        partner = 64 * (NZ - k) - 8 * qq
        if k == 0:
            partner = jnp.where(qq == 0, 256, partner)
        return pl.multiple_of(64 * k + 8 * qq, 8), pl.multiple_of(partner, 8)

    def row_copies(qq):
        copies = []
        for k in range(PAIRS):
            for h, (start, width) in enumerate(zip(pair_rows(k, qq), (lanes_of(k), 256))):
                copies.append(
                    pltpu.make_async_copy(
                        spectra.at[0, :, pl.ds(start, 8), pl.ds(0, width)],
                        rows.at[:, pl.ds(start, 8), pl.ds(0, width)],
                        rows_sem.at[qq, k, h],
                    )
                )
        return copies

    def place(i):
        return (y + i // 2) % (NQ // 2) * 2 + (q + i) % 2

    @pl.loop(0, NQ)
    def _(i):
        for copy in row_copies(place(i)):
            copy.start()

    def kept(start, width, valid):
        block = rows[:, pl.ds(start, 8), pl.ds(0, width)]
        order = lax.broadcasted_iota(jnp.int32, (8, width), 0) + start
        degree = lax.broadcasted_iota(jnp.int32, (8, width), 1)
        keep = degree < jnp.where(valid, jnp.maximum(limits[gx, 0] - order, 1), 0)
        return jnp.where(keep[None], block, 0.0).reshape(48, width)

    def pack(qq):
        for copy in row_copies(qq):
            copy.wait()
        for k in range(PAIRS):
            block = 8 * k + qq
            first, second = pair_rows(k, qq)
            width = lanes_of(k)
            one = kept(first, width, True)
            two = pltpu.roll(kept(second, 256, block > 0), (256 - 8 * block) % 256, 1)
            if width < DEGREES:
                one = jnp.concatenate([one, jnp.zeros((48, DEGREES - width), F32)], axis=1)
            both = jnp.concatenate([one[:, :256], one[:, 256:] + two], axis=1)
            packed[pl.ds(48 * k, 48), :] = both.astype(BF16)
        mixed = jnp.dot(mixer[...], packed[...], preferred_element_type=F32)
        sends[pl.ds(qq * GX, GX)] = mixed.astype(BF16).reshape(GX, 48, DEGREES)

        @pl.when(qq == 0)
        def _():
            alone = kept(256, 256, True).astype(BF16)
            zeros = jnp.zeros((96, 128), BF16)
            spread = jnp.concatenate([alone[:, :128], alone[:, 128:], zeros], axis=0)
            mixed = jnp.dot(mixer[...], spread, preferred_element_type=F32)
            sends_x[...] = mixed.astype(BF16).reshape(GX, 48, 128)

    def spec_copy(x, qq):
        return pltpu.make_async_remote_copy(
            src_ref=sends.at[qq * GX + x],
            dst_ref=recv.at[q, gx],
            send_sem=spec_send,
            recv_sem=spec_recv.at[y],
            device_id=peer(x, qq),
            device_id_type=MESH,
        )

    def spec_arrivals(yy):
        part = recv.at[pl.ds(2 * yy, 2)]
        return pltpu.make_async_copy(part, part, spec_recv.at[yy])

    def spec_departures():
        part = sends.at[pl.ds(0, PEERS - 1)]
        return pltpu.make_async_copy(part, part, spec_send)

    def x_copy(x):
        return pltpu.make_async_remote_copy(
            src_ref=sends_x.at[x],
            dst_ref=recv_x.at[q, gx],
            send_sem=x_send,
            recv_sem=x_recv.at[y],
            device_id=peer(x, 0),
            device_id_type=MESH,
        )

    def x_arrivals(yy):
        part = recv_x.at[pl.ds(2 * yy, 2)]
        return pltpu.make_async_copy(part, part, x_recv.at[yy])

    def x_departures(count):
        part = sends_x.at[pl.ds(0, count)]
        return pltpu.make_async_copy(part, part, x_send)

    def send_spec(qq):
        @pl.loop(0, GX)
        def _(j):
            x = (gx + j) % GX

            @pl.when(x * NQ + qq != me)
            def _():
                spec_copy(x, qq).start()

            @pl.when((x * NQ + qq != me) & (qq == 0))
            def _():
                x_copy(x).start()

    def pieces_of(zb):
        return 4 - zb // 2

    def mine_at(o, t):
        return legendre.at[2 * gx + o, :, pl.ds(128 * t, 128)]

    def leg_piece(o, step, way, t, arriving):
        shift = step + 1 if arriving else step
        zb = (z + NZ - shift) % NZ if way == 0 else (z + shift) % NZ
        onward, backward = (up, down) if way == 0 else (down, up)
        if arriving:
            target = along(backward, jnp.where(zb < PAIRS, q, mirror) if step == 0 else q)
        else:
            target = along(onward, column if step == 0 else q)
        copy = pltpu.make_async_remote_copy(
            src_ref=mine_at(o, t) if step == 0 and not arriving else basis.at[zb, o, t],
            dst_ref=basis.at[zb, o, t],
            send_sem=leg_send.at[o, way, step, t],
            recv_sem=leg_recv.at[o, way, step, t],
            device_id=target,
            device_id_type=MESH,
        )
        return t < pieces_of(zb), copy

    def goes(step, way, t):
        return step < 3 or way == t % 2

    def own_remote(o, t):
        return pltpu.make_async_remote_copy(
            src_ref=mine_at(o, t),
            dst_ref=basis.at[z, o, t],
            send_sem=own_send.at[o, t],
            recv_sem=own_recv.at[o, t],
            device_id=along(z, mirror),
            device_id_type=MESH,
        )

    def own_local(o, t):
        return pltpu.make_async_copy(mine_at(o, t), basis.at[z, o, t], own_recv.at[o, t])

    def own_each(o, remote, local):
        for t in range(4):
            here = t < pieces_of(z)

            @pl.when(here & (column != q))
            def _():
                remote(own_remote(o, t))

            if local is None:
                continue

            @pl.when(here & (column == q))
            def _():
                local(own_local(o, t))

    def leg_first(o):
        for t in range(4):
            for way in range(2):
                here, copy = leg_piece(o, 0, way, t, False)
                pl.when(here)(copy.start)
        own_each(o, lambda c: c.start(), lambda c: c.start())

    def leg_forward(o, step):
        for t in range(4):
            for way in range(2):
                if not goes(step, way, t):
                    continue
                here, arrival = leg_piece(o, step, way, t, True)

                @pl.when(here)
                def _():
                    arrival.wait_recv()
                    if step < 3 and goes(step + 1, way, t):
                        leg_piece(o, step + 1, way, t, False)[1].start()

    limit_copy.wait()
    mixer_copy.wait()
    pack(q)
    pl.semaphore_wait(barrier, PEERS - 1 + 4)
    leg_first(0)
    send_spec(q)
    pltpu.make_async_copy(sends.at[q * GX + gx], recv.at[q, gx], spec_recv.at[y]).start()

    @pl.when(q == 0)
    def _():
        pltpu.make_async_copy(sends_x.at[gx], recv_x.at[0, gx], x_recv.at[0]).start()

    @pl.when(q != 0)
    def _():
        recv_x[...] = jnp.zeros_like(recv_x)

    def pack_and_send(i):
        pack(place(i))
        send_spec(place(i))

    pl.loop(1, 4)(pack_and_send)
    leg_forward(0, 0)
    pl.loop(4, 6)(pack_and_send)
    leg_forward(0, 1)
    leg_first(1)
    pl.loop(6, 8)(pack_and_send)
    leg_forward(0, 2)
    leg_forward(1, 0)
    leg_forward(0, 3)
    leg_forward(1, 1)
    leg_forward(1, 2)
    own_each(0, lambda c: c.wait_recv(), lambda c: c.wait())

    def out_copy(x, qq, what, o):
        return pltpu.make_async_remote_copy(
            src_ref=fd.at[qq, x, what, o],
            dst_ref=field.at[what, o, :, me],
            send_sem=out_send.at[what, o],
            recv_sem=out_recv.at[what, o],
            device_id=peer(x, qq),
            device_id_type=MESH,
        )

    def out_arrivals(what, o):
        part = field.at[what, o]
        return pltpu.make_async_copy(part, part, out_recv.at[what, o])

    def out_departures(what, o):
        part = field.at[what, o, :, pl.ds(0, PEERS - 1)]
        return pltpu.make_async_copy(part, part, out_send.at[what, o])

    def send_out(qq, what, o):
        @pl.loop(0, GX)
        def _(j):
            x = (gx + j) % GX

            @pl.when(x * NQ + qq != me)
            def _():
                out_copy(x, qq, what, o).start()

        @pl.when(qq == q)
        def _():
            pltpu.make_async_copy(
                fd.at[q, gx, what, o], field.at[what, o, :, me], out_recv.at[what, o]
            ).start()

    def low_copy(o):
        return pltpu.make_async_remote_copy(
            src_ref=fd.at[NQ - 1, :, 0, o],
            dst_ref=low.at[o],
            send_sem=end_send.at[0, o],
            recv_sem=end_recv.at[0, o],
            device_id=along(up, q),
            device_id_type=MESH,
        )

    def high_copy(o):
        return pltpu.make_async_remote_copy(
            src_ref=fd.at[0, :, 0, o],
            dst_ref=high.at[o],
            send_sem=end_send.at[1, o],
            recv_sem=end_recv.at[1, o],
            device_id=along(down, q),
            device_id_type=MESH,
        )

    rows384 = lax.broadcasted_iota(jnp.int32, (384, 256), 0)
    pair_of = rows384 % 8 // 2

    def inner_differences(yy, o):
        @pl.when(yy < NQ // 2 - 1)
        def _():
            m = 2 * yy + 1
            outer = fd[pl.ds(m + 1, 2), :, 0, o].astype(F32)
            inner = fd[pl.ds(m - 1, 2), :, 0, o].astype(F32)
            fd[pl.ds(m, 2), :, 1, o] = (0.5 * (outer - inner)).astype(BF16)
            send_out(m, 1, o)
            send_out(m + 1, 1, o)

    def end_differences(o):
        low_copy(o).wait_recv()
        high_copy(o).wait_recv()
        for x in range(GX):
            bottom = fd[0, x, 0, o].astype(F32)
            second = fd[1, x, 0, o].astype(F32)
            before = low[o, x - 1].astype(F32) if x > 0 else 2.0 * bottom - second
            below = jnp.where(z == 0, before, low[o, x].astype(F32))
            fd[0, x, 1, o] = (0.5 * (second - below)).astype(BF16)
            top = fd[NQ - 1, x, 0, o].astype(F32)
            last = fd[NQ - 2, x, 0, o].astype(F32)
            after = high[o, x + 1].astype(F32) if x < GX - 1 else 2.0 * top - last
            above = jnp.where(z == NZ - 1, after, high[o, x].astype(F32))
            fd[NQ - 1, x, 1, o] = (0.5 * (above - last)).astype(BF16)
        send_out(0, 1, o)
        send_out(NQ - 1, 1, o)

    def build_weights(o):
        lane = lax.broadcasted_iota(jnp.int32, (128, DEGREES), 1)
        for k in range(PAIRS):
            block = 8 * k + q
            cut = DEGREES - 8 * block
            one = jnp.concatenate([basis[k, o, t] for t in range(4)], axis=1).astype(F32)
            weights[k, 0:128, :] = jnp.where(lane < cut, one, 0.0).astype(BF16)
            zb = jnp.where(q == 0, NZ - max(k, 1), NZ - 1 - k)
            two = jnp.concatenate([basis[zb, o, t] for t in range(2)], axis=1).astype(F32)
            two = pltpu.roll(two, (256 - 8 * block) % 256, 1)
            two = jnp.where(lane[:, 256:] >= cut, two, 0.0)
            weights[k, 128:256, :] = jnp.concatenate([jnp.zeros((128, 256), F32), two], axis=1).astype(BF16)
        weights_x[...] = jnp.concatenate([basis[PAIRS, o, t] for t in range(2)], axis=0)

    def coefficients(o):
        @pl.loop(0, NQ // 2)
        def _(i):
            yy = (y + NQ // 2 - i) % (NQ // 2)
            two = pl.ds(2 * yy, 2)
            if o == 0:
                spec_arrivals(yy).wait()

                @pl.when(q == 0)
                def _():
                    x_arrivals(yy).wait()

            block = recv[two].reshape(384, DEGREES)
            total = jnp.zeros((384, 256), F32)
            for k in range(PAIRS):
                both = lax.dot_general(block, weights[k], (((1,), (1,)), ((), ())), preferred_element_type=F32)
                total = jnp.where(pair_of == k, both, total)
            extra = lax.dot_general(
                recv_x[two].reshape(384, 128), weights_x[...], (((1,), (1,)), ((), ())), preferred_element_type=F32
            )
            extra = extra[:, :128] + pltpu.roll(extra[:, 128:], 382, 0)
            lower = total[:, :128]
            upper = total[:, 128:] + jnp.where(pair_of[:, :128] == 0, extra, 0.0)
            both = [part.reshape(2, GX, 3, 2, 8, 128)[:, :, :, o] for part in (lower, upper)]
            fd[two, :, 0, o] = jnp.concatenate(both, axis=3).astype(BF16)
            send_out(2 * yy, 0, o)
            send_out(2 * yy + 1, 0, o)

            @pl.when(yy == NQ // 2 - 1)
            def _():
                low_copy(o).start()

            @pl.when(yy == 0)
            def _():
                high_copy(o).start()

            @pl.when(i >= 1)
            def _():
                inner_differences(yy, o)

        inner_differences(y, o)

    build_weights(0)
    coefficients(0)
    leg_forward(1, 3)
    own_each(1, lambda c: c.wait_recv(), lambda c: c.wait())
    build_weights(1)
    end_differences(0)
    coefficients(1)
    end_differences(1)

    def left_copy(o):
        return pltpu.make_async_copy(turned.at[o], left.at[o], left_sem.at[o])

    spec_departures().wait()

    @pl.when(q == 0)
    def _():
        x_departures(GX - 1).wait()

    @pl.when(q != 0)
    def _():
        x_departures(GX).wait()

    for o in range(2):
        low_copy(o).wait_send()
        high_copy(o).wait_send()
        own_each(o, lambda c: c.wait_send(), None)
        for step in range(4):
            for t in range(4):
                for way in range(2):
                    if goes(step, way, t):
                        here, copy = leg_piece(o, step, way, t, False)
                        pl.when(here)(copy.wait_send)

    for o in range(2):
        for what in range(2):
            out_arrivals(what, o).wait()
            for v in range(3):
                block = field[what, o, v].reshape(512, 128)
                turned[o, pl.ds(128 * (3 * what + v), 128), :] = block.T
        left_copy(o).start()

    for o in range(2):
        for what in range(2):
            out_departures(what, o).wait()
        left_copy(o).wait()


def exchange(counts, spectra, legendre, perm):
    return pl.pallas_call(
        exchange_kernel,
        out_shape=jax.ShapeDtypeStruct((2, 768, 512), BF16),
        in_specs=[pl.BlockSpec(memory_space=pl.ANY)] * 4,
        out_specs=pl.BlockSpec(memory_space=pl.ANY),
        scratch_shapes=[
            pltpu.SMEM((GX, 512), jnp.int32),
            pltpu.VMEM((192, 192), BF16),
            pltpu.VMEM((6, 512, 512), F32),
            pltpu.VMEM((192, DEGREES), BF16),
            pltpu.VMEM((PEERS, 48, DEGREES), BF16),
            pltpu.VMEM((NQ, GX, 48, DEGREES), BF16),
            pltpu.VMEM((GX, 48, 128), BF16),
            pltpu.VMEM((NQ, GX, 48, 128), BF16),
            pltpu.VMEM((NZ, 2, 4, 128, 128), BF16),
            pltpu.VMEM((PAIRS, 256, DEGREES), BF16),
            pltpu.VMEM((256, 128), BF16),
            pltpu.VMEM((NQ, GX, 2, 2, 3, 16, 128), BF16),
            pltpu.VMEM((2, GX, 3, 16, 128), BF16),
            pltpu.VMEM((2, GX, 3, 16, 128), BF16),
            pltpu.VMEM((2, 2, 3, PEERS, 16, 128), BF16),
            pltpu.VMEM((2, 768, 512), BF16),
            pltpu.SemaphoreType.DMA,
            pltpu.SemaphoreType.DMA,
            pltpu.SemaphoreType.DMA((NQ, PAIRS, 2)),
            pltpu.SemaphoreType.DMA((2, 4)),
            pltpu.SemaphoreType.DMA((2, 4)),
            pltpu.SemaphoreType.DMA,
            pltpu.SemaphoreType.DMA((NQ // 2,)),
            pltpu.SemaphoreType.DMA,
            pltpu.SemaphoreType.DMA((NQ // 2,)),
            pltpu.SemaphoreType.DMA((2, 2, 4, 4)),
            pltpu.SemaphoreType.DMA((2, 2, 4, 4)),
            pltpu.SemaphoreType.DMA((2, 2)),
            pltpu.SemaphoreType.DMA((2, 2)),
            pltpu.SemaphoreType.DMA((2, 2)),
            pltpu.SemaphoreType.DMA((2, 2)),
            pltpu.SemaphoreType.DMA((2,)),
        ],
        compiler_params=pltpu.CompilerParams(
            collective_id=0, has_side_effects=True, vmem_limit_bytes=57 * 2**20
        ),
        cost_estimate=pl.CostEstimate(flops=2 * 10**9, bytes_accessed=10**7, transcendentals=0),
    )(counts, spectra, legendre, perm)


TILE = 256
STEPS = HALF // TILE
CHUNK = 16


def synthesis_kernel(field, geometry, left, table, out, factors, waves, stage, sems):
    squared = field[0]
    cos_theta = geometry[0]
    sin_theta = geometry[1]
    factors[0] = cos_theta
    factors[1] = sin_theta
    factors[2] = squared * cos_theta * sin_theta
    factors[3] = 0.5 * squared * sin_theta * sin_theta
    factors[4] = 2.0 * squared * cos_theta * cos_theta
    factors[5] = 0.5 * squared * (4.0 * cos_theta * cos_theta + sin_theta * sin_theta)

    def ship(i, h):
        return pltpu.make_async_copy(
            stage.at[i, h],
            out.at[0, :, :, pl.ds(h * HALF + i * TILE, TILE)],
            sems.at[i, h],
        )

    def wide(value):
        return jnp.concatenate([value] * (TILE // 128), axis=1)

    for i in range(STEPS):
        columns = pl.ds(i * TILE, TILE)
        for o in range(2):
            waves[i % 2, o] = jnp.dot(left[o], table[o, :, columns], preferred_element_type=F32)
        for r in range(0, NLAT_W, CHUNK):
            here = pl.ds(r, CHUNK)
            cos_w, sin_w, mix, own, twice, total = (wide(factors[n, here, :]) for n in range(6))
            even = [waves[i % 2, 0, pl.ds(128 * n + r, CHUNK), :] for n in range(6)]
            odd = [waves[i % 2, 1, pl.ds(128 * n + r, CHUNK), :] for n in range(6)]
            for h in range(2):
                flow = [a + b if h == 0 else a - b for a, b in zip(even, odd)]
                radial, polar, azimuth = flow[:3]
                stage[i, h, 0, here, :] = (
                    sin_w * azimuth + mix * polar - radial * (own + flow[3])
                ).astype(BF16)
                stage[i, h, 1, here, :] = (
                    cos_w * azimuth - twice * polar + radial * (mix - flow[4])
                ).astype(BF16)
                stage[i, h, 2, here, :] = (
                    -(cos_w * polar + total * azimuth + radial * (sin_w + flow[5]))
                ).astype(BF16)
        for h in range(2):
            ship(i, h).start()
    for i in range(STEPS):
        for h in range(2):
            ship(i, h).wait()


def synthesis(field, geometry, left, table):
    return pl.pallas_call(
        synthesis_kernel,
        out_shape=jax.ShapeDtypeStruct((1, 3, NLAT_W, LONGITUDE_COUNT), BF16),
        in_specs=[
            pl.BlockSpec(memory_space=pltpu.SMEM),
            pl.BlockSpec(memory_space=pltpu.VMEM),
            pl.BlockSpec(memory_space=pltpu.VMEM),
            pl.BlockSpec(memory_space=pltpu.VMEM),
        ],
        out_specs=pl.BlockSpec(memory_space=pl.ANY),
        scratch_shapes=[
            pltpu.VMEM((6, NLAT_W, 128), F32),
            pltpu.VMEM((2, 2, 768, TILE), F32),
            pltpu.VMEM((STEPS, 2, 3, NLAT_W, TILE), BF16),
            pltpu.SemaphoreType.DMA((STEPS, 2)),
        ],
        compiler_params=pltpu.CompilerParams(vmem_limit_bytes=32 * 2**20),
        cost_estimate=pl.CostEstimate(flops=3 * 10**9, bytes_accessed=7 * 10**6, transcendentals=0),
    )(field, geometry, left, table)


def shards(spectra, legendre, degree_counts):
    perm = jnp.asarray(order_permutation(), BF16)
    table = jnp.asarray(fourier_table(), BF16)
    theta = np.pi * (np.arange(NLAT_W) + (NLAT - NLAT_W) // 2 + 0.5) / NLAT
    geometry = np.repeat(np.stack([np.cos(theta), np.sin(theta)])[:, :, None], 128, axis=2)
    geometry = jnp.asarray(geometry, F32)
    shell = lax.axis_index(("grp", "sub")).astype(F32)
    radius = RADIUS_IN + (shell + 0.5) / SHELLS
    field = ((RADIUS_IN / radius) ** 6).reshape(1)
    left = exchange(degree_counts, spectra, legendre, perm)
    return synthesis(field, geometry, left, table)


def solution(mesh):
    in_specs = (P(("grp", "sub"), None, None, None), P("sub", None, None), P())
    out_specs = P(("grp", "sub"), None, None, None)
    return jax.shard_map(shards, mesh=mesh, in_specs=in_specs, out_specs=out_specs, check_vma=False)
```

time: 71.1 us -> 68.2 us (0.959)
  the two profiles are of different devices: /device:TPU:249 before, /device:TPU:4 now
where the time goes in v3:
time: 68.2 us; the launch traced here: 68.1 us
  Pallas kernels  66.6 us (98%)
  local copies, waits for them, and re-layouts  1.41 us (2%)
    pallas_call x1, Pallas kernels, exchange(): pl.pallas_call(exchange_kernel, out_shape=jax.ShapeDtypeStruct((2, 768, 5...  62.8 us
    pallas_call x1, Pallas kernels, synthesis(): pl.pallas_call(synthesis_kernel, out_shape=jax.ShapeDtypeStruct((1, 3, NL...  3.84 us
    unnamed x6, local copies, waits for them, and re-layouts  1.41 us

profile of v3, /device:TPU:4, one launch (start us, length us, event | category | flops | bytes accessed | tf_op | source)
XLA Modules:
  0.0 68.1 jit_solution(15293577369663343134)
XLA Ops:
  0.1 0.0 copy-start.1
  0.1 0.0 copy-start.2
  0.1 62.8 %shard_map.64.left = bf16[2,768,512]{2,1,0:T(8,128)(2,1)} custom-call(s32[4,512]{1,0:T(4,128)} %counts.1, f32[1,6,512,512]{3,2,1,0:T(8,128)} %spectra.1, bf16[8,128,512]{2,1,0:T(8,128)(2,1)} %legendre.1, bf16[192,192]{1,0:T(8,128)(2,1)} %constant.24.clone.perm), custom_call_target="tpu_custom_call" | custom-call | flops 2000000000 | bytes 10000000 | tf_op jit(solution)/shard_map/pallas_call | solution.py:500
  62.8 0.0 copy-done.1
  62.8 0.0 copy-done.2
  62.9 0.0 copy-start
  62.9 1.4 %copy-done = bf16[2,768,512]{2,1,0:T(8,128)(2,1)S(1)} copy-done((bf16[2,768,512]{2,1,0:T(8,128)(2,1)S(1)}, bf16[2,768,512]{2,1,0:T(8,128)(2,1)}, u32[]{:S(2)}) %copy-start) | copy-done | bytes 1572888
  64.3 3.8 %shard_map.65 = bf16[1,3,128,3072]{3,2,1,0:T(8,128)(2,1)} custom-call(f32[1]{0:T(128)} %bitcast.field, f32[2,128,128]{2,1,0:T(8,128)S(1)} %copy-done.2, bf16[2,768,512]{2,1,0:T(8,128)(2,1)S(1)} %copy-done, bf16[2,512,1536]{2,1,0:T(8,128)(2,1)S(1)} %copy-done.1), custom_call_target="tpu_custom_call" | custom-call | flops 3000000000 | bytes 7000000 | tf_op jit(solution)/shard_map/pallas_call | solution.py:601
Async XLA Ops:
  0.1 62.8 %copy-start.1 = (bf16[2,512,1536]{2,1,0:T(8,128)(2,1)S(1)}, bf16[2,512,1536]{2,1,0:T(8,128)(2,1)}, u32[]{:S(2)}) copy-start(bf16[2,512,1536]{2,1,0:T(8,128)(2,1)} %constant.25.clone.table) | copy-start | bytes 9437188
  0.1 62.8 %copy-start.2 = (f32[2,128,128]{2,1,0:T(8,128)S(1)}, f32[2,128,128]{2,1,0:T(8,128)}, u32[]{:S(2)}) copy-start(f32[2,128,128]{2,1,0:T(8,128)} %constant.26.clone.geometry) | copy-start | bytes 393220
  62.9 1.4 %copy-start = (bf16[2,768,512]{2,1,0:T(8,128)(2,1)S(1)}, bf16[2,768,512]{2,1,0:T(8,128)(2,1)}, u32[]{:S(2)}) copy-start(bf16[2,768,512]{2,1,0:T(8,128)(2,1)} %shard_map.64.left) | copy-start | bytes 4718596

commit v4 on v3

--- a/solution.py
+++ b/solution.py
@@ -265,8 +265,8 @@
         own_each(o, lambda c: c.start(), lambda c: c.start())
 
     def leg_forward(o, step):
-        for t in range(4):
-            for way in range(2):
+        for way in range(2):
+            for t in range(4):
                 if not goes(step, way, t):
                     continue
                 here, arrival = leg_piece(o, step, way, t, True)
@@ -297,23 +297,21 @@
         pack(place(i))
         send_spec(place(i))
 
-    pl.loop(1, 4)(pack_and_send)
+    leg_first(1)
+    pl.loop(1, 8)(pack_and_send)
     leg_forward(0, 0)
-    pl.loop(4, 6)(pack_and_send)
+    leg_forward(1, 0)
     leg_forward(0, 1)
-    leg_first(1)
-    pl.loop(6, 8)(pack_and_send)
+    leg_forward(1, 1)
     leg_forward(0, 2)
-    leg_forward(1, 0)
+    leg_forward(1, 2)
     leg_forward(0, 3)
-    leg_forward(1, 1)
-    leg_forward(1, 2)
     own_each(0, lambda c: c.wait_recv(), lambda c: c.wait())
 
     def out_copy(x, qq, what, o):
         return pltpu.make_async_remote_copy(
             src_ref=fd.at[qq, x, what, o],
-            dst_ref=field.at[what, o, :, me],
+            dst_ref=field.at[what, o, me],
             send_sem=out_send.at[what, o],
             recv_sem=out_recv.at[what, o],
             device_id=peer(x, qq),
@@ -325,7 +323,7 @@
         return pltpu.make_async_copy(part, part, out_recv.at[what, o])
 
     def out_departures(what, o):
-        part = field.at[what, o, :, pl.ds(0, PEERS - 1)]
+        part = field.at[what, o, pl.ds(0, PEERS - 1)]
         return pltpu.make_async_copy(part, part, out_send.at[what, o])
 
     def send_out(qq, what, o):
@@ -340,7 +338,7 @@
         @pl.when(qq == q)
         def _():
             pltpu.make_async_copy(
-                fd.at[q, gx, what, o], field.at[what, o, :, me], out_recv.at[what, o]
+                fd.at[q, gx, what, o], field.at[what, o, me], out_recv.at[what, o]
             ).start()
 
     def low_copy(o):
@@ -419,6 +417,11 @@
                 def _():
                     x_arrivals(yy).wait()
 
+            if o == 1:
+                @pl.when(i == 2)
+                def _():
+                    end_differences(0)
+
             block = recv[two].reshape(384, DEGREES)
             total = jnp.zeros((384, 256), F32)
             for k in range(PAIRS):
@@ -454,7 +457,6 @@
     leg_forward(1, 3)
     own_each(1, lambda c: c.wait_recv(), lambda c: c.wait())
     build_weights(1)
-    end_differences(0)
     coefficients(1)
     end_differences(1)
 
@@ -486,7 +488,7 @@
         for what in range(2):
             out_arrivals(what, o).wait()
             for v in range(3):
-                block = field[what, o, v].reshape(512, 128)
+                block = field[what, o, :, v].reshape(512, 128)
                 turned[o, pl.ds(128 * (3 * what + v), 128), :] = block.T
         left_copy(o).start()
 
@@ -517,7 +519,7 @@
             pltpu.VMEM((NQ, GX, 2, 2, 3, 16, 128), BF16),
             pltpu.VMEM((2, GX, 3, 16, 128), BF16),
             pltpu.VMEM((2, GX, 3, 16, 128), BF16),
-            pltpu.VMEM((2, 2, 3, PEERS, 16, 128), BF16),
+            pltpu.VMEM((2, 2, PEERS, 3, 16, 128), BF16),
             pltpu.VMEM((2, 768, 512), BF16),
             pltpu.SemaphoreType.DMA,
             pltpu.SemaphoreType.DMA,
@@ -537,10 +539,10 @@
             pltpu.SemaphoreType.DMA((2,)),
         ],
         compiler_params=pltpu.CompilerParams(
-            collective_id=0, has_side_effects=True, vmem_limit_bytes=57 * 2**20
+            collective_id=0, has_side_effects=True, vmem_limit_bytes=32 * 2**20
         ),
         cost_estimate=pl.CostEstimate(flops=2 * 10**9, bytes_accessed=10**7, transcendentals=0),
-    )(counts, spectra, legendre, perm)
+    )(*(pltpu.with_memory_space_constraint(a, pltpu.HBM) for a in (counts, spectra, legendre, perm)))
 
 
 TILE = 256

time: 68.2 us -> 60.1 us (0.88)
  the two profiles are of different devices: /device:TPU:4 before, /device:TPU:6 now
where the time goes in v4:
time: 60.1 us; the launch traced here: 59.3 us
  Pallas kernels  59.1 us (98%)
    pallas_call x1, Pallas kernels, exchange(): pl.pallas_call(exchange_kernel, out_shape=jax.ShapeDtypeStruct((2, 768, 5...  55.1 us
    pallas_call x1, Pallas kernels, synthesis(): pl.pallas_call(synthesis_kernel, out_shape=jax.ShapeDtypeStruct((1, 3, NL...  4.04 us

profile of v4, /device:TPU:6, one launch (start us, length us, event | category | flops | bytes accessed | tf_op | source)
XLA Modules:
  0.0 59.3 jit_solution(12532255029913873882)
XLA Ops:
  0.1 0.0 copy-start
  0.1 0.0 copy-start.1
  0.1 55.1 %shard_map.64.left = bf16[2,768,512]{2,1,0:T(8,128)(2,1)S(1)} custom-call(s32[4,512]{1,0:T(4,128)} %counts.1, f32[1,6,512,512]{3,2,1,0:T(8,128)} %spectra.1, bf16[8,128,512]{2,1,0:T(8,128)(2,1)} %legendre.1, bf16[192,192]{1,0:T(8,128)(2,1)} %constant.24.clone.perm), custom_call_target="tpu_custom_call" | custom-call | flops 2000000000 | bytes 10000000 | tf_op jit(solution)/shard_map/pallas_call | solution.py:502
  55.2 0.0 copy-done
  55.2 0.0 copy-done.1
  55.2 4.0 %shard_map.65 = bf16[1,3,128,3072]{3,2,1,0:T(8,128)(2,1)} custom-call(f32[1]{0:T(128)} %bitcast.field, f32[2,128,128]{2,1,0:T(8,128)S(1)} %copy-done.1, bf16[2,768,512]{2,1,0:T(8,128)(2,1)S(1)} %shard_map.64.left, bf16[2,512,1536]{2,1,0:T(8,128)(2,1)S(1)} %copy-done), custom_call_target="tpu_custom_call" | custom-call | flops 3000000000 | bytes 7000000 | tf_op jit(solution)/shard_map/pallas_call | solution.py:603
Async XLA Ops:
  0.1 55.1 %copy-start = (bf16[2,512,1536]{2,1,0:T(8,128)(2,1)S(1)}, bf16[2,512,1536]{2,1,0:T(8,128)(2,1)}, u32[]{:S(2)}) copy-start(bf16[2,512,1536]{2,1,0:T(8,128)(2,1)} %constant.25.clone.table) | copy-start | bytes 9437188
  0.1 55.1 %copy-start.1 = (f32[2,128,128]{2,1,0:T(8,128)S(1)}, f32[2,128,128]{2,1,0:T(8,128)}, u32[]{:S(2)}) copy-start(f32[2,128,128]{2,1,0:T(8,128)} %constant.26.clone.geometry) | copy-start | bytes 393220

commit v5 on v4

--- a/solution.py
+++ b/solution.py
@@ -192,7 +192,7 @@
     def send_spec(qq):
         @pl.loop(0, GX)
         def _(j):
-            x = (gx + j) % GX
+            x = (gx + j + q) % GX
 
             @pl.when(x * NQ + qq != me)
             def _():
@@ -297,8 +297,8 @@
         pack(place(i))
         send_spec(place(i))
 
+    pl.loop(1, 8)(pack_and_send)
     leg_first(1)
-    pl.loop(1, 8)(pack_and_send)
     leg_forward(0, 0)
     leg_forward(1, 0)
     leg_forward(0, 1)
@@ -329,7 +329,7 @@
     def send_out(qq, what, o):
         @pl.loop(0, GX)
         def _(j):
-            x = (gx + j) % GX
+            x = (gx + j + q) % GX
 
             @pl.when(x * NQ + qq != me)
             def _():
@@ -571,10 +571,12 @@
     def wide(value):
         return jnp.concatenate([value] * (TILE // 128), axis=1)
 
-    for i in range(STEPS):
+    def transform(i):
         columns = pl.ds(i * TILE, TILE)
         for o in range(2):
             waves[i % 2, o] = jnp.dot(left[o], table[o, :, columns], preferred_element_type=F32)
+
+    def finish(i):
         for r in range(0, NLAT_W, CHUNK):
             here = pl.ds(r, CHUNK)
             cos_w, sin_w, mix, own, twice, total = (wide(factors[n, here, :]) for n in range(6))
@@ -594,6 +596,12 @@
                 ).astype(BF16)
         for h in range(2):
             ship(i, h).start()
+
+    transform(0)
+    for i in range(STEPS):
+        if i + 1 < STEPS:
+            transform(i + 1)
+        finish(i)
     for i in range(STEPS):
         for h in range(2):
             ship(i, h).wait()

time: 60.1 us -> 59.9 us (level)
  the two profiles are of different devices: /device:TPU:6 before, /device:TPU:1 now
where the time goes in v5:
time: 59.9 us
  Pallas kernels  59.8 us (100%)
    pallas_call x1, Pallas kernels, exchange(): pl.pallas_call(exchange_kernel, out_shape=jax.ShapeDtypeStruct((2, 768, 5...  55.7 us
    pallas_call x1, Pallas kernels, synthesis(): pl.pallas_call(synthesis_kernel, out_shape=jax.ShapeDtypeStruct((1, 3, NL...  4.03 us

profile of v5, /device:TPU:1, one launch (start us, length us, event | category | flops | bytes accessed | tf_op | source)
XLA Modules:
  0.0 59.9 jit_solution(18322974063983600551)
XLA Ops:
  0.1 0.0 copy-start
  0.1 0.0 copy-start.1
  0.1 55.7 %shard_map.64.left = bf16[2,768,512]{2,1,0:T(8,128)(2,1)S(1)} custom-call(s32[4,512]{1,0:T(4,128)} %counts.1, f32[1,6,512,512]{3,2,1,0:T(8,128)} %spectra.1, bf16[8,128,512]{2,1,0:T(8,128)(2,1)} %legendre.1, bf16[192,192]{1,0:T(8,128)(2,1)} %constant.24.clone.perm), custom_call_target="tpu_custom_call" | custom-call | flops 2000000000 | bytes 10000000 | tf_op jit(solution)/shard_map/pallas_call | solution.py:502
  55.8 0.0 copy-done
  55.8 0.0 copy-done.1
  55.8 4.0 %shard_map.65 = bf16[1,3,128,3072]{3,2,1,0:T(8,128)(2,1)} custom-call(f32[1]{0:T(128)} %bitcast.field, f32[2,128,128]{2,1,0:T(8,128)S(1)} %copy-done.1, bf16[2,768,512]{2,1,0:T(8,128)(2,1)S(1)} %shard_map.64.left, bf16[2,512,1536]{2,1,0:T(8,128)(2,1)S(1)} %copy-done), custom_call_target="tpu_custom_call" | custom-call | flops 3000000000 | bytes 7000000 | tf_op jit(solution)/shard_map/pallas_call | solution.py:611
Async XLA Ops:
  0.1 55.8 %copy-start = (bf16[2,512,1536]{2,1,0:T(8,128)(2,1)S(1)}, bf16[2,512,1536]{2,1,0:T(8,128)(2,1)}, u32[]{:S(2)}) copy-start(bf16[2,512,1536]{2,1,0:T(8,128)(2,1)} %constant.25.clone.table) | copy-start | bytes 9437188
  0.1 55.8 %copy-start.1 = (f32[2,128,128]{2,1,0:T(8,128)S(1)}, f32[2,128,128]{2,1,0:T(8,128)}, u32[]{:S(2)}) copy-start(f32[2,128,128]{2,1,0:T(8,128)} %constant.26.clone.geometry) | copy-start | bytes 393220
